TPU v7x, 32 devices: a whole 2x2x4 slice. The times are simulated.
32 devices in a mesh: rows: 4 (over z), segment: 4 (over y, x), tm: 2 (over core).
Axes of the slice: x: 2, y: 2, z: 4, core: 2. Of those that a mesh axis runs over, the one named last changes fastest.
Arguments:
- latents: bfloat16 [4, 8, 8, 128, 128], P(None, 'tm', 'rows'), may hold values from -40 to 40
- conv_first: bfloat16 [4, 3, 3, 3, 128, 128], P('segment'), may hold values from -0.109375 to 0.109375
- conv_second: bfloat16 [4, 3, 3, 3, 128, 128], P('segment'), may hold values from -0.109375 to 0.109375
- gain_first: bfloat16 [4, 128], P('segment'), may hold values from 0.099609375 to 1.8984375
- bias_first: bfloat16 [4, 128], P('segment'), may hold values from -1 to 1
- gain_second: bfloat16 [4, 128], P('segment'), may hold values from 0.099609375 to 1.8984375
- bias_second: bfloat16 [4, 128], P('segment'), may hold values from -1 to 1
Outputs:
- decoded: bfloat16 [4, 8, 8, 128, 128], P('segment', 'tm', 'rows')
All inputs are finite; a program needn't handle non-finite values.
Results may differ from a plain program's by a relative error of at most 0.022.
Values may be sent and summed in bfloat16 or wider, within the bound.
A program may use at most 64 MiB of HBM per device.

v0:
```python
import jax
import jax.numpy as jnp
from jax import lax
from jax.sharding import PartitionSpec as P

GROUPS = 32


EPS = 1e-06


def passed_along(value, axis, steps):
    count = lax.axis_size(axis)
    initial, last = (max(0, -steps), min(count, count - steps))
    return lax.ppermute(value, axis, [(source, source + steps) for source in range(initial, last)])


def padded_2(block, sides, width):
    for axis, dim in sides:
        count = lax.axis_size(axis)
        forward = [(i, i + 1) for i in range(count - 1)]
        backward = [(target, source) for source, target in forward]
        low = lax.ppermute(
            lax.slice_in_dim(block, block.shape[dim] - width, None, axis=dim), axis, forward
        )
        high = lax.ppermute(lax.slice_in_dim(block, 0, width, axis=dim), axis, backward)
        block = jnp.concatenate([low, block, high], axis=dim)
    return block


def normalize(values, norm_gain, norm_bias):
    frames, rows_here, columns, channels = values.shape
    width_group = channels // GROUPS
    grouped = values.astype(jnp.float32).reshape(frames, rows_here, columns, GROUPS, width_group)
    totals = lax.psum(
        (jnp.sum(grouped, axis=(0, 1, 2, 4)), jnp.sum(grouped * grouped, axis=(0, 1, 2, 4))), "rows"
    )
    members = frames * rows_here * lax.axis_size("rows") * columns * width_group
    average = totals[0] / members
    squares = totals[1] / members
    inverse = lax.rsqrt(squares - average * average + EPS)
    scaled = (grouped - average[:, None]) * inverse[:, None]
    scaled = scaled.reshape(values.shape) * norm_gain.astype(jnp.float32) + norm_bias.astype(
        jnp.float32
    )
    return jax.nn.silu(scaled).astype(jnp.bfloat16)


def convolve(active, kernel):
    previous = passed_along(active[-2:], "tm", 1)
    extended = jnp.concatenate([previous, active], axis=0)
    padded = padded_2(extended, (("rows", 1),), 1)
    padded = jnp.pad(padded, ((0, 0), (0, 0), (1, 1), (0, 0)))
    result = lax.conv_general_dilated(
        padded[None],
        kernel,
        (1, 1, 1),
        "VALID",
        dimension_numbers=("NDHWC", "DHWIO", "NDHWC"),
        preferred_element_type=jnp.float32,
    )
    return result[0]


def residual_block(values, params):
    first, second, gain_one, bias_one, gain_two, bias_two = params
    active = normalize(values, gain_one, bias_one)
    hidden = convolve(active, first).astype(jnp.bfloat16)
    active = normalize(hidden, gain_two, bias_two)
    return (values.astype(jnp.float32) + convolve(active, second)).astype(jnp.bfloat16)


def body(latents, conv_first, conv_second, gain_first, bias_first, gain_second, bias_second):
    segments = lax.axis_size("segment")
    micro = latents.shape[0]
    per_segment = micro // segments
    position = lax.axis_index("segment")
    small = jnp.stack([gain_first, bias_first, gain_second, bias_second], axis=1)
    small = lax.all_gather(small, "segment", axis=0, tiled=True)
    first = lax.all_gather(conv_first, "segment", axis=0, tiled=True)
    second = lax.all_gather(conv_second, "segment", axis=0, tiled=True)
    outs = []
    for index in range(per_segment):
        values = lax.dynamic_index_in_dim(
            latents, position * per_segment + index, 0, keepdims=False
        )
        for layer in range(first.shape[0]):
            gains = small[layer]
            values = residual_block(
                values, (first[layer], second[layer], gains[0], gains[1], gains[2], gains[3])
            )
        outs.append(values)
    return jnp.stack(outs)


def solution(mesh):
    in_specs = (
        P(None, "tm", "rows", None, None),
        P("segment", None, None, None, None, None),
        P("segment", None, None, None, None, None),
        P("segment", None),
        P("segment", None),
        P("segment", None),
        P("segment", None),
    )
    out_specs = P("segment", "tm", "rows", None, None)
    return jax.shard_map(body, mesh=mesh, in_specs=in_specs, out_specs=out_specs, check_vma=False)
```

profile of v0, /device:TPU:0, one launch (start us, length us, event | category | flops | bytes accessed | tf_op | source)
XLA Modules:
  0.0 296.4 jit_solution(6094731690513591556)
XLA Ops:
  8.6 13.5 %all-reduce.15 = (f32[32]{0:T(128)S(1)}, f32[32]{0:T(128)S(1)}) all-reduce(f32[32]{0:T(128)S(1)} %reduce_sum.195, f32[32]{0:T(128)S(1)} %reduce_sum.189), channel_id=1, replica_groups=mesh['rows'=4,'segment'=4,'tm'=2] {'rows'}, use_global_device_ids=true, to_apply=%region_5.6 | all-reduce | flops 64 | bytes 512 | tf_op jit(solution)/shard_map/psum | solution.py:35
  22.5 8.1 %all_gather.9 = bf16[4,4,128]{2,1,0:T(4,128)(2,1)S(1)} all-gather(bf16[1,4,128]{2,1,0:T(4,128)(2,1)S(1)} %pad_maximum_fusion.8), channel_id=1, replica_groups=mesh['rows'=4,'segment'=4,'tm'=2] {'segment'}, dimensions={0}, use_global_device_ids=true | all-gather | bytes 5120 | tf_op jit(solution)/shard_map/all_gather | solution.py:79
  30.9 1.3 collective-permute-start
  32.2 1.0 collective-permute-done
  33.2 1.3 collective-permute-start.1
  34.5 1.3 collective-permute-start.2
  35.8 3.6 %collective-permute-done.1 = bf16[6,1,128,128]{3,2,1,0:T(8,128)(2,1)S(1)} collective-permute-done((bf16[6,1,128,128]{3,2,1,0:T(8,128)(2,1)S(1)}, bf16[6,1,128,128]{3,2,1,0:T(8,128)(2,1)S(1)}, u32[]{:S(2)}, u32[]{:S(2)}) %collective-permute-start.1) | collective-permute-done | bytes 196640 | tf_op jit(solution)/shard_map/ppermute | solution.py:23
  39.4 4.1 %collective-permute-done.2 = bf16[6,1,128,128]{3,2,1,0:T(8,128)(2,1)S(1)} collective-permute-done((bf16[6,1,128,128]{3,2,1,0:T(8,128)(2,1)S(1)}, bf16[6,1,128,128]{3,2,1,0:T(8,128)(2,1)S(1)}, u32[]{:S(2)}, u32[]{:S(2)}) %collective-permute-start.2) | collective-permute-done | bytes 196640 | tf_op jit(solution)/shard_map/ppermute | solution.py:26
  44.6 14.6 %all-gather.3.cloned.1.call-done = bf16[4,3,3,3,128,128]{5,4,3,2,1,0:T(8,128)(2,1)} async-done(((bf16[1,3,3,3,128,128]{5,4,3,2,1,0:T(8,128)(2,1)}), bf16[4,3,3,3,128,128]{5,4,3,2,1,0:T(8,128)(2,1)}) %all-gather.3.cloned.1.call-update) | async-done | bytes 3538960 | tf_op jit(solution)/shard_map/all_gather | solution.py:80
  59.2 3.3 %fusion.81 = (f32[128]{0:T(128)S(1)}, f32[128]{0:T(128)S(1)}, bf16[4,2,8,17,128]{4,2,3,1,0:T(8,128)(2,1)S(1)}) fusion(pred[8,17]{0,1:T(8,128)(4,1)S(1)} %copy-done.5, bf16[4,3,3,3,128,128]{5,4,3,2,1,0:T(8,128)(2,1)} %all-gather.3.cloned.1.call-done, bf16[6,4,1,7,2,128]{5,3,4,1,0,2:T(8,128)(2,1)S(1)} %slice.249, bf16[6,4,1,8,17,128]{5,3,4,1,0,2:T(8,128)(2,1)S(1)} %copy.62), kind=kOutput, calls=%fused_computation.137 | convolution fusion | flops 966508288 | bytes 2086024 | tf_op jit(solution)/shard_map/conv_general_dilated | solution.py:54
  63.0 11.7 %all-reduce.14 = (f32[32]{0:T(128)S(1)}, f32[32]{0:T(128)S(1)}) all-reduce(f32[32]{0:T(128)S(1)} %reduce_sum.204, f32[32]{0:T(128)S(1)} %reduce_sum.201), channel_id=1, replica_groups=mesh['rows'=4,'segment'=4,'tm'=2] {'rows'}, use_global_device_ids=true, to_apply=%region_11.12 | all-reduce | flops 64 | bytes 512 | tf_op jit(solution)/shard_map/psum | solution.py:35
  75.7 1.3 collective-permute-start.3
  78.0 1.3 collective-permute-start.4
  79.3 1.3 collective-permute-start.5
  80.6 3.6 %collective-permute-done.4 = bf16[6,1,128,128]{3,2,1,0:T(8,128)(2,1)S(1)} collective-permute-done((bf16[6,1,128,128]{3,2,1,0:T(8,128)(2,1)S(1)}, bf16[6,1,128,128]{3,2,1,0:T(8,128)(2,1)S(1)}, u32[]{:S(2)}, u32[]{:S(2)}) %collective-permute-start.4) | collective-permute-done | bytes 196640 | tf_op jit(solution)/shard_map/ppermute | solution.py:23
  84.3 4.1 %collective-permute-done.5 = bf16[6,1,128,128]{3,2,1,0:T(8,128)(2,1)S(1)} collective-permute-done((bf16[6,1,128,128]{3,2,1,0:T(8,128)(2,1)S(1)}, bf16[6,1,128,128]{3,2,1,0:T(8,128)(2,1)S(1)}, u32[]{:S(2)}, u32[]{:S(2)}) %collective-permute-start.5) | collective-permute-done | bytes 196640 | tf_op jit(solution)/shard_map/ppermute | solution.py:26
  89.4 18.9 %all-gather.5.cloned.1.call-done = bf16[4,3,3,3,128,128]{5,4,3,2,1,0:T(8,128)(2,1)} async-done(((bf16[1,3,3,3,128,128]{5,4,3,2,1,0:T(8,128)(2,1)}), bf16[4,3,3,3,128,128]{5,4,3,2,1,0:T(8,128)(2,1)}) %all-gather.5.cloned.1.call-update) | async-done | bytes 3538960 | tf_op jit(solution)/shard_map/all_gather | solution.py:81
  108.4 3.3 %convolution_select_fusion.6 = f32[4,2,8,17,128]{4,2,3,1,0:T(8,128)S(1)} fusion(bf16[6,4,1,7,2,128]{5,3,4,1,0,2:T(8,128)(2,1)S(1)} %slice.257, bf16[6,4,1,8,17,128]{5,3,4,1,0,2:T(8,128)(2,1)S(1)} %copy.67, bf16[4,3,3,3,128,128]{5,4,3,2,1,0:T(8,128)(2,1)} %all-gather.5.cloned.1.call-done, pred[8,17]{0,1:T(8,128)(4,1)S(1)} %copy-done.5), kind=kOutput, calls=%fused_computation.18 | convolution fusion | flops 965533696 | bytes 2363528 | tf_op jit(solution)/shard_map/conv_general_dilated | solution.py:54
  112.6 11.7 %all-reduce.13 = (f32[32]{0:T(128)S(1)}, f32[32]{0:T(128)S(1)}) all-reduce(f32[32]{0:T(128)S(1)} %reduce_sum.216, f32[32]{0:T(128)S(1)} %reduce_sum.210), channel_id=1, replica_groups=mesh['rows'=4,'segment'=4,'tm'=2] {'rows'}, use_global_device_ids=true, to_apply=%region_17.18 | all-reduce | flops 64 | bytes 512 | tf_op jit(solution)/shard_map/psum | solution.py:35
  124.9 1.3 collective-permute-start.6
  126.3 1.0 collective-permute-done.6
  127.3 1.3 collective-permute-start.7
  128.6 1.5 collective-permute-start.8
  130.0 3.5 %collective-permute-done.7 = bf16[6,1,128,128]{3,2,1,0:T(8,128)(2,1)S(1)} collective-permute-done((bf16[6,1,128,128]{3,2,1,0:T(8,128)(2,1)S(1)}, bf16[6,1,128,128]{3,2,1,0:T(8,128)(2,1)S(1)}, u32[]{:S(2)}, u32[]{:S(2)}) %collective-permute-start.7) | collective-permute-done | bytes 196640 | tf_op jit(solution)/shard_map/ppermute | solution.py:23
  133.5 4.1 %collective-permute-done.8 = bf16[6,1,128,128]{3,2,1,0:T(8,128)(2,1)S(1)} collective-permute-done((bf16[6,1,128,128]{3,2,1,0:T(8,128)(2,1)S(1)}, bf16[6,1,128,128]{3,2,1,0:T(8,128)(2,1)S(1)}, u32[]{:S(2)}, u32[]{:S(2)}) %collective-permute-start.8) | collective-permute-done | bytes 196640 | tf_op jit(solution)/shard_map/ppermute | solution.py:26
  138.7 3.3 %fusion.84 = (f32[128]{0:T(128)S(1)}, f32[128]{0:T(128)S(1)}, bf16[4,2,8,17,128]{4,2,3,1,0:T(8,128)(2,1)S(1)}) fusion(pred[8,17]{0,1:T(8,128)(4,1)S(1)} %copy-done.5, bf16[4,3,3,3,128,128]{5,4,3,2,1,0:T(8,128)(2,1)} %all-gather.3.cloned.1.call-done, bf16[6,4,1,7,2,128]{5,3,4,1,0,2:T(8,128)(2,1)S(1)} %slice.265, bf16[6,4,1,8,17,128]{5,3,4,1,0,2:T(8,128)(2,1)S(1)} %copy.72), kind=kOutput, calls=%fused_computation.140 | convolution fusion | flops 966508288 | bytes 2086024 | tf_op jit(solution)/shard_map/conv_general_dilated | solution.py:54
  142.5 8.9 %all-reduce.12 = (f32[32]{0:T(128)S(1)}, f32[32]{0:T(128)S(1)}) all-reduce(f32[32]{0:T(128)S(1)} %reduce_sum.225, f32[32]{0:T(128)S(1)} %reduce_sum.219), channel_id=1, replica_groups=mesh['rows'=4,'segment'=4,'tm'=2] {'rows'}, use_global_device_ids=true, to_apply=%region_23.24 | all-reduce | flops 64 | bytes 512 | tf_op jit(solution)/shard_map/psum | solution.py:35
  152.4 1.3 collective-permute-start.9
  153.7 1.0 collective-permute-done.9
  154.7 3.4 %collective-permute-start.10 = (bf16[6,1,128,128]{3,2,1,0:T(8,128)(2,1)S(1)}, bf16[6,1,128,128]{3,2,1,0:T(8,128)(2,1)S(1)}, u32[]{:S(2)}, u32[]{:S(2)}) collective-permute-start(bf16[6,1,128,128]{3,2,1,0:T(8,128)(2,1)S(1)} %get-tuple-element.50), channel_id=1, source_target_pairs={{0,8},{8,16},{16,24},{1,9},{9,17},{17,25},{2,10},{10,18},{18,26},{... | collective-permute-start | bytes 589832 | tf_op jit(solution)/shard_map/ppermute | solution.py:23
  158.1 1.3 collective-permute-start.11
  159.4 3.3 %collective-permute-done.10 = bf16[6,1,128,128]{3,2,1,0:T(8,128)(2,1)S(1)} collective-permute-done((bf16[6,1,128,128]{3,2,1,0:T(8,128)(2,1)S(1)}, bf16[6,1,128,128]{3,2,1,0:T(8,128)(2,1)S(1)}, u32[]{:S(2)}, u32[]{:S(2)}) %collective-permute-start.10) | collective-permute-done | bytes 196640 | tf_op jit(solution)/shard_map/ppermute | solution.py:23
  162.7 4.1 %collective-permute-done.11 = bf16[6,1,128,128]{3,2,1,0:T(8,128)(2,1)S(1)} collective-permute-done((bf16[6,1,128,128]{3,2,1,0:T(8,128)(2,1)S(1)}, bf16[6,1,128,128]{3,2,1,0:T(8,128)(2,1)S(1)}, u32[]{:S(2)}, u32[]{:S(2)}) %collective-permute-start.11) | collective-permute-done | bytes 196640 | tf_op jit(solution)/shard_map/ppermute | solution.py:26
  167.9 3.3 %convolution_select_fusion.4 = f32[4,2,8,17,128]{4,2,3,1,0:T(8,128)S(1)} fusion(bf16[6,4,1,7,2,128]{5,3,4,1,0,2:T(8,128)(2,1)S(1)} %slice.273, bf16[6,4,1,8,17,128]{5,3,4,1,0,2:T(8,128)(2,1)S(1)} %copy.77, bf16[4,3,3,3,128,128]{5,4,3,2,1,0:T(8,128)(2,1)} %all-gather.5.cloned.1.call-done, pred[8,17]{0,1:T(8,128)(4,1)S(1)} %copy-done.5), kind=kOutput, calls=%fused_computation.16 | convolution fusion | flops 965533696 | bytes 2363528 | tf_op jit(solution)/shard_map/conv_general_dilated | solution.py:54
  172.1 8.7 %all-reduce.11 = (f32[32]{0:T(128)S(1)}, f32[32]{0:T(128)S(1)}) all-reduce(f32[32]{0:T(128)S(1)} %reduce_sum.234, f32[32]{0:T(128)S(1)} %reduce_sum.231), channel_id=1, replica_groups=mesh['rows'=4,'segment'=4,'tm'=2] {'rows'}, use_global_device_ids=true, to_apply=%region_29.30 | all-reduce | flops 64 | bytes 512 | tf_op jit(solution)/shard_map/psum | solution.py:35
  181.4 1.3 collective-permute-start.12
  183.7 3.6 %collective-permute-start.13 = (bf16[6,1,128,128]{3,2,1,0:T(8,128)(2,1)S(1)}, bf16[6,1,128,128]{3,2,1,0:T(8,128)(2,1)S(1)}, u32[]{:S(2)}, u32[]{:S(2)}) collective-permute-start(bf16[6,1,128,128]{3,2,1,0:T(8,128)(2,1)S(1)} %get-tuple-element.48), channel_id=1, source_target_pairs={{0,8},{8,16},{16,24},{1,9},{9,17},{17,25},{2,10},{10,18},{18,26},{... | collective-permute-start | bytes 589832 | tf_op jit(solution)/shard_map/ppermute | solution.py:23
  187.3 1.3 collective-permute-start.14
  188.6 3.3 %collective-permute-done.13 = bf16[6,1,128,128]{3,2,1,0:T(8,128)(2,1)S(1)} collective-permute-done((bf16[6,1,128,128]{3,2,1,0:T(8,128)(2,1)S(1)}, bf16[6,1,128,128]{3,2,1,0:T(8,128)(2,1)S(1)}, u32[]{:S(2)}, u32[]{:S(2)}) %collective-permute-start.13) | collective-permute-done | bytes 196640 | tf_op jit(solution)/shard_map/ppermute | solution.py:23
  192.0 4.1 %collective-permute-done.14 = bf16[6,1,128,128]{3,2,1,0:T(8,128)(2,1)S(1)} collective-permute-done((bf16[6,1,128,128]{3,2,1,0:T(8,128)(2,1)S(1)}, bf16[6,1,128,128]{3,2,1,0:T(8,128)(2,1)S(1)}, u32[]{:S(2)}, u32[]{:S(2)}) %collective-permute-start.14) | collective-permute-done | bytes 196640 | tf_op jit(solution)/shard_map/ppermute | solution.py:26
  197.2 3.3 %fusion.87 = (f32[128]{0:T(128)S(1)}, f32[128]{0:T(128)S(1)}, bf16[4,2,8,17,128]{4,2,3,1,0:T(8,128)(2,1)S(1)}) fusion(pred[8,17]{0,1:T(8,128)(4,1)S(1)} %copy-done.5, bf16[4,3,3,3,128,128]{5,4,3,2,1,0:T(8,128)(2,1)} %all-gather.3.cloned.1.call-done, bf16[6,4,1,7,2,128]{5,3,4,1,0,2:T(8,128)(2,1)S(1)} %slice.281, bf16[6,4,1,8,17,128]{5,3,4,1,0,2:T(8,128)(2,1)S(1)} %copy.82), kind=kOutput, calls=%fused_computation.143 | convolution fusion | flops 966508288 | bytes 2086024 | tf_op jit(solution)/shard_map/conv_general_dilated | solution.py:54
  200.9 8.9 %all-reduce.10 = (f32[32]{0:T(128)S(1)}, f32[32]{0:T(128)S(1)}) all-reduce(f32[32]{0:T(128)S(1)} %reduce_sum.291, f32[32]{0:T(128)S(1)} %reduce_sum.288), channel_id=1, replica_groups=mesh['rows'=4,'segment'=4,'tm'=2] {'rows'}, use_global_device_ids=true, to_apply=%region_35.36 | all-reduce | flops 64 | bytes 512 | tf_op jit(solution)/shard_map/psum | solution.py:35
  210.8 1.3 collective-permute-start.15
  213.1 3.6 %collective-permute-start.16 = (bf16[6,1,128,128]{3,2,1,0:T(8,128)(2,1)S(1)}, bf16[6,1,128,128]{3,2,1,0:T(8,128)(2,1)S(1)}, u32[]{:S(2)}, u32[]{:S(2)}) collective-permute-start(bf16[6,1,128,128]{3,2,1,0:T(8,128)(2,1)S(1)} %get-tuple-element.46), channel_id=1, source_target_pairs={{0,8},{8,16},{16,24},{1,9},{9,17},{17,25},{2,10},{10,18},{18,26},{... | collective-permute-start | bytes 589832 | tf_op jit(solution)/shard_map/ppermute | solution.py:23
  216.8 1.3 collective-permute-start.17
  218.1 3.3 %collective-permute-done.16 = bf16[6,1,128,128]{3,2,1,0:T(8,128)(2,1)S(1)} collective-permute-done((bf16[6,1,128,128]{3,2,1,0:T(8,128)(2,1)S(1)}, bf16[6,1,128,128]{3,2,1,0:T(8,128)(2,1)S(1)}, u32[]{:S(2)}, u32[]{:S(2)}) %collective-permute-start.16) | collective-permute-done | bytes 196640 | tf_op jit(solution)/shard_map/ppermute | solution.py:23
  221.4 4.1 %collective-permute-done.17 = bf16[6,1,128,128]{3,2,1,0:T(8,128)(2,1)S(1)} collective-permute-done((bf16[6,1,128,128]{3,2,1,0:T(8,128)(2,1)S(1)}, bf16[6,1,128,128]{3,2,1,0:T(8,128)(2,1)S(1)}, u32[]{:S(2)}, u32[]{:S(2)}) %collective-permute-start.17) | collective-permute-done | bytes 196640 | tf_op jit(solution)/shard_map/ppermute | solution.py:26
  226.6 3.3 %convolution_select_fusion.2 = f32[4,2,8,17,128]{4,2,3,1,0:T(8,128)S(1)} fusion(bf16[6,4,1,7,2,128]{5,3,4,1,0,2:T(8,128)(2,1)S(1)} %slice.289, bf16[6,4,1,8,17,128]{5,3,4,1,0,2:T(8,128)(2,1)S(1)} %copy.87, bf16[4,3,3,3,128,128]{5,4,3,2,1,0:T(8,128)(2,1)} %all-gather.5.cloned.1.call-done, pred[8,17]{0,1:T(8,128)(4,1)S(1)} %copy-done.5), kind=kOutput, calls=%fused_computation.14 | convolution fusion | flops 965533696 | bytes 2363528 | tf_op jit(solution)/shard_map/conv_general_dilated | solution.py:54
  230.8 8.6 %all-reduce.9 = (f32[32]{0:T(128)S(1)}, f32[32]{0:T(128)S(1)}) all-reduce(f32[32]{0:T(128)S(1)} %reduce_sum.297, f32[32]{0:T(128)S(1)} %reduce_sum.294), channel_id=1, replica_groups=mesh['rows'=4,'segment'=4,'tm'=2] {'rows'}, use_global_device_ids=true, to_apply=%region_41.42 | all-reduce | flops 64 | bytes 512 | tf_op jit(solution)/shard_map/psum | solution.py:35
  240.1 1.3 collective-permute-start.18
  241.4 1.0 collective-permute-done.18
  242.4 3.6 %collective-permute-start.19 = (bf16[6,1,128,128]{3,2,1,0:T(8,128)(2,1)S(1)}, bf16[6,1,128,128]{3,2,1,0:T(8,128)(2,1)S(1)}, u32[]{:S(2)}, u32[]{:S(2)}) collective-permute-start(bf16[6,1,128,128]{3,2,1,0:T(8,128)(2,1)S(1)} %get-tuple-element.44), channel_id=1, source_target_pairs={{0,8},{8,16},{16,24},{1,9},{9,17},{17,25},{2,10},{10,18},{18,26},{... | collective-permute-start | bytes 589832 | tf_op jit(solution)/shard_map/ppermute | solution.py:23
  246.1 1.3 collective-permute-start.20
  247.4 3.3 %collective-permute-done.19 = bf16[6,1,128,128]{3,2,1,0:T(8,128)(2,1)S(1)} collective-permute-done((bf16[6,1,128,128]{3,2,1,0:T(8,128)(2,1)S(1)}, bf16[6,1,128,128]{3,2,1,0:T(8,128)(2,1)S(1)}, u32[]{:S(2)}, u32[]{:S(2)}) %collective-permute-start.19) | collective-permute-done | bytes 196640 | tf_op jit(solution)/shard_map/ppermute | solution.py:23
  250.7 4.1 %collective-permute-done.20 = bf16[6,1,128,128]{3,2,1,0:T(8,128)(2,1)S(1)} collective-permute-done((bf16[6,1,128,128]{3,2,1,0:T(8,128)(2,1)S(1)}, bf16[6,1,128,128]{3,2,1,0:T(8,128)(2,1)S(1)}, u32[]{:S(2)}, u32[]{:S(2)}) %collective-permute-start.20) | collective-permute-done | bytes 196640 | tf_op jit(solution)/shard_map/ppermute | solution.py:26
  255.9 3.3 %fusion.90 = (f32[128]{0:T(128)S(1)}, f32[128]{0:T(128)S(1)}, bf16[4,2,8,17,128]{4,2,3,1,0:T(8,128)(2,1)S(1)}) fusion(pred[8,17]{0,1:T(8,128)(4,1)S(1)} %copy-done.5, bf16[4,3,3,3,128,128]{5,4,3,2,1,0:T(8,128)(2,1)} %all-gather.3.cloned.1.call-done, bf16[6,4,1,7,2,128]{5,3,4,1,0,2:T(8,128)(2,1)S(1)} %slice.297, bf16[6,4,1,8,17,128]{5,3,4,1,0,2:T(8,128)(2,1)S(1)} %copy.92), kind=kOutput, calls=%fused_computation.146 | convolution fusion | flops 966508288 | bytes 2086024 | tf_op jit(solution)/shard_map/conv_general_dilated | solution.py:54
  259.7 8.7 %all-reduce.8 = (f32[32]{0:T(128)S(1)}, f32[32]{0:T(128)S(1)}) all-reduce(f32[32]{0:T(128)S(1)} %reduce_sum.303, f32[32]{0:T(128)S(1)} %reduce_sum.300), channel_id=1, replica_groups=mesh['rows'=4,'segment'=4,'tm'=2] {'rows'}, use_global_device_ids=true, to_apply=%region_47.48 | all-reduce | flops 64 | bytes 512 | tf_op jit(solution)/shard_map/psum | solution.py:35
  269.4 1.3 collective-permute-start.21
  270.7 1.0 collective-permute-done.21
  271.7 3.6 %collective-permute-start.22 = (bf16[6,1,128,128]{3,2,1,0:T(8,128)(2,1)S(1)}, bf16[6,1,128,128]{3,2,1,0:T(8,128)(2,1)S(1)}, u32[]{:S(2)}, u32[]{:S(2)}) collective-permute-start(bf16[6,1,128,128]{3,2,1,0:T(8,128)(2,1)S(1)} %get-tuple-element.42), channel_id=1, source_target_pairs={{0,8},{8,16},{16,24},{1,9},{9,17},{17,25},{2,10},{10,18},{18,26},{... | collective-permute-start | bytes 589832 | tf_op jit(solution)/shard_map/ppermute | solution.py:23
  275.3 1.6 collective-permute-start.23
  276.8 3.1 %collective-permute-done.22 = bf16[6,1,128,128]{3,2,1,0:T(8,128)(2,1)S(1)} collective-permute-done((bf16[6,1,128,128]{3,2,1,0:T(8,128)(2,1)S(1)}, bf16[6,1,128,128]{3,2,1,0:T(8,128)(2,1)S(1)}, u32[]{:S(2)}, u32[]{:S(2)}) %collective-permute-start.22) | collective-permute-done | bytes 196640 | tf_op jit(solution)/shard_map/ppermute | solution.py:23
  279.9 4.1 %collective-permute-done.23 = bf16[6,1,128,128]{3,2,1,0:T(8,128)(2,1)S(1)} collective-permute-done((bf16[6,1,128,128]{3,2,1,0:T(8,128)(2,1)S(1)}, bf16[6,1,128,128]{3,2,1,0:T(8,128)(2,1)S(1)}, u32[]{:S(2)}, u32[]{:S(2)}) %collective-permute-start.23) | collective-permute-done | bytes 196640 | tf_op jit(solution)/shard_map/ppermute | solution.py:26
  285.1 3.3 %convolution_select_fusion = f32[4,2,8,17,128]{4,2,3,1,0:T(8,128)S(1)} fusion(bf16[6,4,1,7,2,128]{5,3,4,1,0,2:T(8,128)(2,1)S(1)} %slice.305, bf16[6,4,1,8,17,128]{5,3,4,1,0,2:T(8,128)(2,1)S(1)} %copy.97, bf16[4,3,3,3,128,128]{5,4,3,2,1,0:T(8,128)(2,1)} %all-gather.5.cloned.1.call-done, pred[8,17]{0,1:T(8,128)(4,1)S(1)} %copy-done.5), kind=kOutput, calls=%fused_computation.12 | convolution fusion | flops 965533696 | bytes 2363528 | tf_op jit(solution)/shard_map/conv_general_dilated | solution.py:54
  (178 shorter events, 25.3 us)
Async XLA Ops:
  6.5 1.5 copy-start
  6.5 15.9 %copy-start.1 = (bf16[1,128]{1,0:T(2,128)(2,1)S(1)}, bf16[1,128]{1,0:T(2,128)(2,1)}, u32[]{:S(2)}) copy-start(bf16[1,128]{1,0:T(2,128)(2,1)} %param.13) | copy-start | bytes 772
  6.5 16.0 %copy-start.2 = (bf16[1,128]{1,0:T(2,128)(2,1)S(1)}, bf16[1,128]{1,0:T(2,128)(2,1)}, u32[]{:S(2)}) copy-start(bf16[1,128]{1,0:T(2,128)(2,1)} %param.12) | copy-start | bytes 772
  6.5 16.0 %copy-start.3 = (bf16[1,128]{1,0:T(2,128)(2,1)S(1)}, bf16[1,128]{1,0:T(2,128)(2,1)}, u32[]{:S(2)}) copy-start(bf16[1,128]{1,0:T(2,128)(2,1)} %param.11) | copy-start | bytes 772
  6.5 16.0 %copy-start.4 = (bf16[1,128]{1,0:T(2,128)(2,1)S(1)}, bf16[1,128]{1,0:T(2,128)(2,1)}, u32[]{:S(2)}) copy-start(bf16[1,128]{1,0:T(2,128)(2,1)} %param.10) | copy-start | bytes 772
  6.5 52.7 %all-gather.3.cloned.1.call-start = ((), (), s32[]{:S(2)}) async-start(), calls=%async_computation | async-start | bytes 4423680 | tf_op jit(solution)/shard_map/all_gather | solution.py:80
  7.3 101.1 %all-gather.5.cloned.1.call-start = ((), (), s32[]{:S(2)}) async-start(), calls=%async_computation.1 | async-start | bytes 4423680 | tf_op jit(solution)/shard_map/all_gather | solution.py:81
  30.9 2.3 collective-permute-start
  33.2 6.2 %collective-permute-start.1 = (bf16[6,1,128,128]{3,2,1,0:T(8,128)(2,1)S(1)}, bf16[6,1,128,128]{3,2,1,0:T(8,128)(2,1)S(1)}, u32[]{:S(2)}, u32[]{:S(2)}) collective-permute-start(bf16[6,1,128,128]{3,2,1,0:T(8,128)(2,1)S(1)} %get-tuple-element.56), channel_id=1, source_target_pairs={{0,8},{8,16},{16,24},{1,9},{9,17},{17,25},{2,10},{10,18},{18,26},{... | collective-permute-start | bytes 589832 | tf_op jit(solution)/shard_map/ppermute | solution.py:23
  34.5 9.1 %collective-permute-start.2 = (bf16[6,1,128,128]{3,2,1,0:T(8,128)(2,1)S(1)}, bf16[6,1,128,128]{3,2,1,0:T(8,128)(2,1)S(1)}, u32[]{:S(2)}, u32[]{:S(2)}) collective-permute-start(bf16[6,1,128,128]{3,2,1,0:T(8,128)(2,1)S(1)} %get-tuple-element.57), channel_id=1, source_target_pairs={{8,0},{16,8},{24,16},{9,1},{17,9},{25,17},{10,2},{18,10},{26,18},{... | collective-permute-start | bytes 589832 | tf_op jit(solution)/shard_map/ppermute | solution.py:26
  44.1 15.1 %copy-start.5 = (pred[8,17]{0,1:T(8,128)(4,1)S(1)}, pred[8,17]{0,1:T(8,128)(4,1)}, u32[]{:S(2)}) copy-start(pred[8,17]{0,1:T(8,128)(4,1)} %constant.110) | copy-start | bytes 412
  75.7 2.3 collective-permute-start.3
  78.0 6.2 %collective-permute-start.4 = (bf16[6,1,128,128]{3,2,1,0:T(8,128)(2,1)S(1)}, bf16[6,1,128,128]{3,2,1,0:T(8,128)(2,1)S(1)}, u32[]{:S(2)}, u32[]{:S(2)}) collective-permute-start(bf16[6,1,128,128]{3,2,1,0:T(8,128)(2,1)S(1)} %get-tuple-element.54), channel_id=1, source_target_pairs={{0,8},{8,16},{16,24},{1,9},{9,17},{17,25},{2,10},{10,18},{18,26},{... | collective-permute-start | bytes 589832 | tf_op jit(solution)/shard_map/ppermute | solution.py:23
  79.3 9.1 %collective-permute-start.5 = (bf16[6,1,128,128]{3,2,1,0:T(8,128)(2,1)S(1)}, bf16[6,1,128,128]{3,2,1,0:T(8,128)(2,1)S(1)}, u32[]{:S(2)}, u32[]{:S(2)}) collective-permute-start(bf16[6,1,128,128]{3,2,1,0:T(8,128)(2,1)S(1)} %get-tuple-element.55), channel_id=1, source_target_pairs={{8,0},{16,8},{24,16},{9,1},{17,9},{25,17},{10,2},{18,10},{26,18},{... | collective-permute-start | bytes 589832 | tf_op jit(solution)/shard_map/ppermute | solution.py:26
  124.9 2.3 collective-permute-start.6
  127.3 6.2 %collective-permute-start.7 = (bf16[6,1,128,128]{3,2,1,0:T(8,128)(2,1)S(1)}, bf16[6,1,128,128]{3,2,1,0:T(8,128)(2,1)S(1)}, u32[]{:S(2)}, u32[]{:S(2)}) collective-permute-start(bf16[6,1,128,128]{3,2,1,0:T(8,128)(2,1)S(1)} %get-tuple-element.52), channel_id=1, source_target_pairs={{0,8},{8,16},{16,24},{1,9},{9,17},{17,25},{2,10},{10,18},{18,26},{... | collective-permute-start | bytes 589832 | tf_op jit(solution)/shard_map/ppermute | solution.py:23
  128.6 9.1 %collective-permute-start.8 = (bf16[6,1,128,128]{3,2,1,0:T(8,128)(2,1)S(1)}, bf16[6,1,128,128]{3,2,1,0:T(8,128)(2,1)S(1)}, u32[]{:S(2)}, u32[]{:S(2)}) collective-permute-start(bf16[6,1,128,128]{3,2,1,0:T(8,128)(2,1)S(1)} %get-tuple-element.53), channel_id=1, source_target_pairs={{8,0},{16,8},{24,16},{9,1},{17,9},{25,17},{10,2},{18,10},{26,18},{... | collective-permute-start | bytes 589832 | tf_op jit(solution)/shard_map/ppermute | solution.py:26
  152.4 2.3 collective-permute-start.9
  154.7 8.0 %collective-permute-start.10 = (bf16[6,1,128,128]{3,2,1,0:T(8,128)(2,1)S(1)}, bf16[6,1,128,128]{3,2,1,0:T(8,128)(2,1)S(1)}, u32[]{:S(2)}, u32[]{:S(2)}) collective-permute-start(bf16[6,1,128,128]{3,2,1,0:T(8,128)(2,1)S(1)} %get-tuple-element.50), channel_id=1, source_target_pairs={{0,8},{8,16},{16,24},{1,9},{9,17},{17,25},{2,10},{10,18},{18,26},{... | collective-permute-start | bytes 589832 | tf_op jit(solution)/shard_map/ppermute | solution.py:23
  158.1 8.8 %collective-permute-start.11 = (bf16[6,1,128,128]{3,2,1,0:T(8,128)(2,1)S(1)}, bf16[6,1,128,128]{3,2,1,0:T(8,128)(2,1)S(1)}, u32[]{:S(2)}, u32[]{:S(2)}) collective-permute-start(bf16[6,1,128,128]{3,2,1,0:T(8,128)(2,1)S(1)} %get-tuple-element.51), channel_id=1, source_target_pairs={{8,0},{16,8},{24,16},{9,1},{17,9},{25,17},{10,2},{18,10},{26,18},{... | collective-permute-start | bytes 589832 | tf_op jit(solution)/shard_map/ppermute | solution.py:26
  181.4 2.3 collective-permute-start.12
  183.7 8.3 %collective-permute-start.13 = (bf16[6,1,128,128]{3,2,1,0:T(8,128)(2,1)S(1)}, bf16[6,1,128,128]{3,2,1,0:T(8,128)(2,1)S(1)}, u32[]{:S(2)}, u32[]{:S(2)}) collective-permute-start(bf16[6,1,128,128]{3,2,1,0:T(8,128)(2,1)S(1)} %get-tuple-element.48), channel_id=1, source_target_pairs={{0,8},{8,16},{16,24},{1,9},{9,17},{17,25},{2,10},{10,18},{18,26},{... | collective-permute-start | bytes 589832 | tf_op jit(solution)/shard_map/ppermute | solution.py:23
  187.3 8.8 %collective-permute-start.14 = (bf16[6,1,128,128]{3,2,1,0:T(8,128)(2,1)S(1)}, bf16[6,1,128,128]{3,2,1,0:T(8,128)(2,1)S(1)}, u32[]{:S(2)}, u32[]{:S(2)}) collective-permute-start(bf16[6,1,128,128]{3,2,1,0:T(8,128)(2,1)S(1)} %get-tuple-element.49), channel_id=1, source_target_pairs={{8,0},{16,8},{24,16},{9,1},{17,9},{25,17},{10,2},{18,10},{26,18},{... | collective-permute-start | bytes 589832 | tf_op jit(solution)/shard_map/ppermute | solution.py:26
  210.8 2.3 collective-permute-start.15
  213.1 8.3 %collective-permute-start.16 = (bf16[6,1,128,128]{3,2,1,0:T(8,128)(2,1)S(1)}, bf16[6,1,128,128]{3,2,1,0:T(8,128)(2,1)S(1)}, u32[]{:S(2)}, u32[]{:S(2)}) collective-permute-start(bf16[6,1,128,128]{3,2,1,0:T(8,128)(2,1)S(1)} %get-tuple-element.46), channel_id=1, source_target_pairs={{0,8},{8,16},{16,24},{1,9},{9,17},{17,25},{2,10},{10,18},{18,26},{... | collective-permute-start | bytes 589832 | tf_op jit(solution)/shard_map/ppermute | solution.py:23
  216.8 8.8 %collective-permute-start.17 = (bf16[6,1,128,128]{3,2,1,0:T(8,128)(2,1)S(1)}, bf16[6,1,128,128]{3,2,1,0:T(8,128)(2,1)S(1)}, u32[]{:S(2)}, u32[]{:S(2)}) collective-permute-start(bf16[6,1,128,128]{3,2,1,0:T(8,128)(2,1)S(1)} %get-tuple-element.47), channel_id=1, source_target_pairs={{8,0},{16,8},{24,16},{9,1},{17,9},{25,17},{10,2},{18,10},{26,18},{... | collective-permute-start | bytes 589832 | tf_op jit(solution)/shard_map/ppermute | solution.py:26
  240.1 2.3 collective-permute-start.18
  242.4 8.3 %collective-permute-start.19 = (bf16[6,1,128,128]{3,2,1,0:T(8,128)(2,1)S(1)}, bf16[6,1,128,128]{3,2,1,0:T(8,128)(2,1)S(1)}, u32[]{:S(2)}, u32[]{:S(2)}) collective-permute-start(bf16[6,1,128,128]{3,2,1,0:T(8,128)(2,1)S(1)} %get-tuple-element.44), channel_id=1, source_target_pairs={{0,8},{8,16},{16,24},{1,9},{9,17},{17,25},{2,10},{10,18},{18,26},{... | collective-permute-start | bytes 589832 | tf_op jit(solution)/shard_map/ppermute | solution.py:23
  246.1 8.8 %collective-permute-start.20 = (bf16[6,1,128,128]{3,2,1,0:T(8,128)(2,1)S(1)}, bf16[6,1,128,128]{3,2,1,0:T(8,128)(2,1)S(1)}, u32[]{:S(2)}, u32[]{:S(2)}) collective-permute-start(bf16[6,1,128,128]{3,2,1,0:T(8,128)(2,1)S(1)} %get-tuple-element.45), channel_id=1, source_target_pairs={{8,0},{16,8},{24,16},{9,1},{17,9},{25,17},{10,2},{18,10},{26,18},{... | collective-permute-start | bytes 589832 | tf_op jit(solution)/shard_map/ppermute | solution.py:26
  269.4 2.3 collective-permute-start.21
  271.7 8.3 %collective-permute-start.22 = (bf16[6,1,128,128]{3,2,1,0:T(8,128)(2,1)S(1)}, bf16[6,1,128,128]{3,2,1,0:T(8,128)(2,1)S(1)}, u32[]{:S(2)}, u32[]{:S(2)}) collective-permute-start(bf16[6,1,128,128]{3,2,1,0:T(8,128)(2,1)S(1)} %get-tuple-element.42), channel_id=1, source_target_pairs={{0,8},{8,16},{16,24},{1,9},{9,17},{17,25},{2,10},{10,18},{18,26},{... | collective-permute-start | bytes 589832 | tf_op jit(solution)/shard_map/ppermute | solution.py:23
  275.3 8.8 %collective-permute-start.23 = (bf16[6,1,128,128]{3,2,1,0:T(8,128)(2,1)S(1)}, bf16[6,1,128,128]{3,2,1,0:T(8,128)(2,1)S(1)}, u32[]{:S(2)}, u32[]{:S(2)}) collective-permute-start(bf16[6,1,128,128]{3,2,1,0:T(8,128)(2,1)S(1)} %get-tuple-element.43), channel_id=1, source_target_pairs={{8,0},{16,8},{24,16},{9,1},{17,9},{25,17},{10,2},{18,10},{26,18},{... | collective-permute-start | bytes 589832 | tf_op jit(solution)/shard_map/ppermute | solution.py:26
Sparse Core Ops, SparseCore 0:
  9.2 49.9 all-gather.2
  61.1 47.2 all-gather.4
where the time goes:
time: 297 us; the launch traced here: 296 us
  waiting for transfers between devices  103 us (35%)
  blocking collectives  88.7 us (30%)
  starting transfers between devices  43 us (14%)
  matrix products  26.5 us (9%)
  between operations  14.5 us (5%)
  local copies, waits for them, and re-layouts  13.6 us (5%)
  other arithmetic  7.41 us (2%)
    psum x8, blocking collectives, normalize(): lax.psum((jnp.sum(grouped, axis=(0, 1, 2, 4)), jnp.sum(grouped * grouped,...  80.6 us
    ppermute x8, waiting for transfers between devices, padded_2(): lax.ppermute(lax.slice_in_dim(block, 0, width, axis=dim), axis, backward)  33 us
    ppermute x8, waiting for transfers between devices, padded_2(): lax.ppermute(lax.slice_in_dim(block, block.shape[dim] - width, None, axis...  27.2 us
    conv_general_dilated x8, matrix products, convolve(): lax.conv_general_dilated(padded[None], kernel, (1, 1, 1), 'VALID', dimens...  26.5 us
    ppermute x8, starting transfers between devices, padded_2(): lax.ppermute(lax.slice_in_dim(block, block.shape[dim] - width, None, axis...  21.7 us
    all_gather x1, waiting for transfers between devices, body(): second = lax.all_gather(conv_second, 'segment', axis=0, tiled=True)  18.9 us
    all_gather x1, waiting for transfers between devices, body(): first = lax.all_gather(conv_first, 'segment', axis=0, tiled=True)  14.6 us
    ppermute x8, starting transfers between devices, padded_2(): lax.ppermute(lax.slice_in_dim(block, 0, width, axis=dim), axis, backward)  10.8 us
  transfers between devices with their start and end apart: 26, of which 26 were waited for; matrix products, arithmetic and copies ran while one was open for 3% of the time, Pallas kernels for 0%

commit v1 on v0

--- a/solution.py
+++ b/solution.py
@@ -1,6 +1,10 @@
+import functools
+
 import jax
 import jax.numpy as jnp
 from jax import lax
+from jax.experimental import pallas as pl
+from jax.experimental.pallas import tpu as pltpu
 from jax.sharding import PartitionSpec as P
 
 GROUPS = 32
@@ -70,7 +74,7 @@
     return (values.astype(jnp.float32) + convolve(active, second)).astype(jnp.bfloat16)
 
 
-def body(latents, conv_first, conv_second, gain_first, bias_first, gain_second, bias_second):
+def plain_body(latents, conv_first, conv_second, gain_first, bias_first, gain_second, bias_second):
     segments = lax.axis_size("segment")
     micro = latents.shape[0]
     per_segment = micro // segments
@@ -93,6 +97,433 @@
     return jnp.stack(outs)
 
 
+MESH = pl.DeviceIdType.MESH
+ROWS = 16
+
+
+def group_sums(values):
+    lanes = values.shape[-1]
+    lane = lax.broadcasted_iota(jnp.int32, values.shape, 1)
+    values = values + jnp.where(
+        lax.rem(lane, 2) == 0, pltpu.roll(values, lanes - 1, 1), pltpu.roll(values, 1, 1)
+    )
+    return values + jnp.where(
+        lax.rem(lane, 4) < 2, pltpu.roll(values, lanes - 2, 1), pltpu.roll(values, 2, 1)
+    )
+
+
+def tap_block(weights, dt, dy, dx, channels):
+    if dt < 0 or dt > 2:
+        return jnp.zeros((channels, channels), jnp.bfloat16)
+    return weights[dt, dy, dx]
+
+
+def decode_kernel(
+    count,
+    latents,
+    first,
+    second,
+    small,
+    out,
+    staged,
+    turned,
+    values,
+    hidden,
+    sibling,
+    edges,
+    stats,
+    active,
+    own_sem,
+    in_send,
+    in_recv,
+    stat_send,
+    stat_recv,
+    edge_send,
+    edge_recv,
+    sib_send,
+    sib_recv,
+    out_send,
+    out_recv,
+    free_sem,
+):
+    frames, height, width, channels = staged.shape
+    local_rows = height // count
+    both = 2 * height
+    row = lax.axis_index("rows")
+    segment = lax.axis_index("segment")
+    span = lax.axis_index("tm")
+    members = frames * height * width * count * (channels // GROUPS)
+
+    def at(rows_index, tm_index):
+        return {"rows": rows_index, "tm": tm_index}
+
+    barrier = pltpu.get_barrier_semaphore()
+    for k in range(count):
+        other = lax.rem(row + k, count)
+        if k:
+            pl.semaphore_signal(barrier, inc=1, device_id=at(other, span), device_id_type=MESH)
+        pl.semaphore_signal(barrier, inc=1, device_id=at(other, 1 - span), device_id_type=MESH)
+    pl.semaphore_wait(barrier, 2 * count - 1)
+
+    def incoming(k, me, to):
+        return pltpu.make_async_remote_copy(
+            src_ref=latents.at[segment, :, :, pl.ds(pl.multiple_of(to * width, width), width)],
+            dst_ref=staged.at[:, pl.ds(me * local_rows, local_rows)],
+            send_sem=in_send.at[k],
+            recv_sem=in_recv.at[me],
+            device_id=at(to, span),
+            device_id_type=MESH,
+        )
+
+    for k in range(1, count):
+        incoming(k, row, lax.rem(row + k, count)).start()
+    own = pltpu.make_async_copy(
+        latents.at[segment, :, :, pl.ds(pl.multiple_of(row * width, width), width)],
+        staged.at[:, pl.ds(row * local_rows, local_rows)],
+        own_sem,
+    )
+    own.start()
+    own.wait()
+    for k in range(1, count):
+        other = lax.rem(row + k, count)
+        incoming(k, other, row).wait_recv()
+
+    for f in range(frames):
+        turned[f] = staged[f].astype(jnp.float32).reshape(height * width, channels)
+    zero = jnp.zeros((height, channels), jnp.float32)
+
+    def turn(x, carry):
+        total, squares = carry
+        for q in range(2):
+            tile = jnp.concatenate(
+                [turned[q + 2 * p, pl.ds(x, height, stride=width)] for p in range(2)], axis=0
+            )
+            values[q, x] = tile.astype(jnp.bfloat16)
+            total = total + tile[:height] + tile[height:]
+            tile = tile * tile
+            squares = squares + tile[:height] + tile[height:]
+        return total, squares
+
+    partial = lax.fori_loop(0, width, turn, (zero, zero), unroll=4)
+    for k in range(1, count):
+        incoming(k, row, lax.rem(row + k, count)).wait_send()
+
+    def stat_copy(par, k, me, to, tm_from, tm_to):
+        slot = tm_from * count + me
+        cross = 0 if tm_from is tm_to else count
+        return pltpu.make_async_remote_copy(
+            src_ref=stats.at[par, slot],
+            dst_ref=stats.at[par, slot],
+            send_sem=stat_send.at[par, k + cross],
+            recv_sem=stat_recv.at[par, slot],
+            device_id=at(to, tm_to),
+            device_id_type=MESH,
+        )
+
+    def edge_copy(par, source, side, tm_from, tm_to, to):
+        return pltpu.make_async_remote_copy(
+            src_ref=source.at[:, width - 1 if side == 0 else 0],
+            dst_ref=edges.at[par, side, tm_from],
+            send_sem=edge_send.at[par, side, tm_to],
+            recv_sem=edge_recv.at[par, side, tm_from],
+            device_id=at(to, tm_to),
+            device_id_type=MESH,
+        )
+
+    def sib_copy(par, source):
+        return pltpu.make_async_remote_copy(
+            src_ref=source,
+            dst_ref=sibling.at[par],
+            send_sem=sib_send.at[par],
+            recv_sem=sib_recv.at[par],
+            device_id=at(row, 1),
+            device_id_type=MESH,
+        )
+
+    def each_send(par, source, act):
+        for k in range(1, count):
+            act(stat_copy(par, k, row, lax.rem(row + k, count), span, span))
+
+        @pl.when(span == 0)
+        def _():
+            for k in range(count):
+                act(stat_copy(par, k, row, lax.rem(row + k, count), 0, 1))
+
+        for side, there in ((0, row < count - 1), (1, row > 0)):
+
+            @pl.when(there)
+            def _(side=side):
+                to = row + 1 if side == 0 else row - 1
+                act(edge_copy(par, source, side, span, span, to))
+
+                @pl.when(span == 0)
+                def _():
+                    act(edge_copy(par, source, side, 0, 1, to))
+
+        @pl.when(span == 0)
+        def _():
+            act(sib_copy(par, source))
+
+    def exchange(par, source, partial):
+        index = lax.broadcasted_iota(jnp.int32, (8, channels), 0)
+        total = jnp.sum(partial[0], axis=0, keepdims=True)
+        squares = jnp.sum(partial[1], axis=0, keepdims=True)
+        stats[par, span * count + row] = jnp.where(
+            index == 0, total, jnp.where(index == 1, squares, 0.0)
+        )
+        each_send(par, source, lambda copy: copy.start())
+
+    def finish_sends(par, source):
+        each_send(par, source, lambda copy: copy.wait_send())
+
+    def receive(par, source):
+        for side, there in ((0, row > 0), (1, row < count - 1)):
+
+            @pl.when(there)
+            def _(side=side):
+                edge_copy(par, source, side, span, span, row).wait_recv()
+
+                @pl.when(span == 1)
+                def _():
+                    edge_copy(par, source, side, 0, 1, row).wait_recv()
+
+        @pl.when(span == 1)
+        def _():
+            sib_copy(par, source).wait_recv()
+            for k in range(count):
+                stat_copy(par, k, lax.rem(row + k, count), row, 0, 1).wait_recv()
+
+        for k in range(1, count):
+            stat_copy(par, k, lax.rem(row + k, count), row, span, span).wait_recv()
+
+    def moments(par, base, gain):
+        total = stats[par, base]
+        for k in range(1, count):
+            total = total + stats[par, base + k]
+        total = group_sums(total) / members
+        average = total[0:1]
+        return average, lax.rsqrt(total[1:2] - average * average + EPS) * gain
+
+    def activate(par, source, gain, bias):
+        mine = moments(par, span * count, gain)
+        before = moments(par, 0, gain)
+        later = span > 0
+        index = lax.broadcasted_iota(jnp.int32, (1, height, channels), 1)
+
+        def silu(tile, moment):
+            half = ((tile - moment[0]) * moment[1] + bias) * 0.5
+            return half + half * jnp.tanh(half)
+
+        def shifted(a, dy):
+            if dy == 0:
+                return jnp.where(index == 0, 0.0, pltpu.roll(a, 1, 1))
+            if dy == 2:
+                return jnp.where(index == height - 1, 0.0, pltpu.roll(a, height - 1, 1))
+            return a
+
+        def put(q, where, size, tile, older, valid):
+            a = silu(tile.astype(jnp.float32), mine).reshape(2 * size, height, channels)
+            b = silu(older.astype(jnp.float32)[:, height:], before)
+            b = jnp.where(later, b, 0.0)
+            if valid is not None:
+                a = jnp.where(valid, a, 0.0)
+                b = jnp.where(valid, b, 0.0)
+            for dy in range(3):
+                now = shifted(a, dy).reshape(size, both, channels)
+                old = shifted(b, dy)
+                active[2 + q, dy, where] = now.astype(jnp.bfloat16)
+                active[q, dy, where] = jnp.concatenate([old, now[:, :height]], axis=1).astype(
+                    jnp.bfloat16
+                )
+
+        step = min(8, width)
+
+        @pl.loop(0, width // step)
+        def _(i):
+            x = i * step
+            for q in range(2):
+                put(
+                    q,
+                    pl.ds(x + 1, step),
+                    step,
+                    source[q, pl.ds(x, step)],
+                    sibling[par, q, pl.ds(x, step)],
+                    None,
+                )
+
+        for side, there in ((0, row > 0), (1, row < count - 1)):
+            for q in range(2):
+                put(
+                    q,
+                    pl.ds(0 if side == 0 else width + 1, 1),
+                    1,
+                    edges[par, side, span, q][None],
+                    edges[par, side, 0, q][None],
+                    there,
+                )
+
+    def convolution(weights, store):
+        step = width
+        partial = None
+        for x in range(0, width, step):
+            left, right = [], []
+            for dy in range(3):
+                for dx in range(3):
+                    for k in (1, 2, 0, 3):
+                        left.append(
+                            active[k, dy, x + dx : x + dx + step].reshape(step * both, channels)
+                        )
+                        right.append(
+                            jnp.concatenate(
+                                [
+                                    tap_block(weights, k - q, dy, dx, channels)
+                                    for q in range(2)
+                                ],
+                                axis=1,
+                            )
+                        )
+            result = jnp.dot(
+                jnp.concatenate(left, axis=1),
+                jnp.concatenate(right, axis=0),
+                preferred_element_type=jnp.float32,
+            )
+            for q in range(2):
+                tile = store(
+                    q, x, step, result[:, q * channels : (q + 1) * channels].reshape(
+                        step, both, channels
+                    )
+                )
+                tile = tile.astype(jnp.float32).reshape(-1, height, channels)
+                total, squares = jnp.sum(tile, axis=0), jnp.sum(tile * tile, axis=0)
+                if partial is None:
+                    partial = (total, squares)
+                else:
+                    partial = (partial[0] + total, partial[1] + squares)
+        return partial
+
+    def store_hidden(q, x, step, tile):
+        tile = tile.astype(jnp.bfloat16)
+        hidden[q, x : x + step] = tile
+        return tile
+
+    def store_values(q, x, step, tile):
+        tile = (values[q, x : x + step].astype(jnp.float32) + tile).astype(jnp.bfloat16)
+        values[q, x : x + step] = tile
+        return tile
+
+    def give(when):
+        @pl.when((span == 1) & when)
+        def _():
+            pl.semaphore_signal(free_sem, inc=1, device_id=at(row, 0), device_id_type=MESH)
+
+    def take(when):
+        @pl.when((span == 0) & when)
+        def _():
+            pl.semaphore_wait(free_sem, 1)
+
+    layers = first.shape[0]
+    exchange(0, values, partial)
+
+    @pl.loop(0, layers)
+    def _(layer):
+        receive(0, values)
+        give(layer > 0)
+        activate(0, values, small[layer, 0:1], small[layer, 1:2])
+        partial = convolution(first.at[layer], store_hidden)
+        finish_sends(0, values)
+        take(layer > 0)
+        exchange(1, hidden, partial)
+        receive(1, hidden)
+        give(layer < layers - 1)
+        activate(1, hidden, small[layer, 2:3], small[layer, 3:4])
+        partial = convolution(second.at[layer], store_values)
+        finish_sends(1, hidden)
+
+        @pl.when(layer < layers - 1)
+        def _():
+            take(layer >= 0)
+            exchange(0, values, partial)
+
+    for q in range(2):
+        whole = values[q].astype(jnp.float32)
+        for p in range(2):
+            turned[q + 2 * p] = whole[:, p * height : (p + 1) * height].reshape(
+                height * width, channels
+            )
+    for f in range(frames):
+        for y in range(height):
+            staged[f, y] = turned[f, pl.ds(y, width, stride=height)].astype(jnp.bfloat16)
+
+    def outgoing(k, me, to):
+        return pltpu.make_async_remote_copy(
+            src_ref=staged.at[:, pl.ds(to * local_rows, local_rows)],
+            dst_ref=out.at[0, :, :, pl.ds(pl.multiple_of(me * width, width), width)],
+            send_sem=out_send.at[k],
+            recv_sem=out_recv.at[me],
+            device_id=at(to, span),
+            device_id_type=MESH,
+        )
+
+    for k in range(1, count):
+        outgoing(k, row, lax.rem(row + k, count)).start()
+    own = pltpu.make_async_copy(
+        staged.at[:, pl.ds(row * local_rows, local_rows)],
+        out.at[0, :, :, pl.ds(pl.multiple_of(row * width, width), width)],
+        own_sem,
+    )
+    own.start()
+    own.wait()
+    for k in range(1, count):
+        other = lax.rem(row + k, count)
+        outgoing(k, other, row).wait_recv()
+        outgoing(k, row, other).wait_send()
+
+
+def body(latents, conv_first, conv_second, gain_first, bias_first, gain_second, bias_second):
+    micro, frames, local_rows, columns, channels = latents.shape
+    count = lax.axis_size("rows")
+    width = columns // count
+    height = local_rows * count
+    small = jnp.stack([gain_first, bias_first, gain_second, bias_second], axis=1)
+    small = lax.all_gather(small, "segment", axis=0, tiled=True).astype(jnp.float32)
+    first = lax.all_gather(conv_first, "segment", axis=0, tiled=True)
+    second = lax.all_gather(conv_second, "segment", axis=0, tiled=True)
+    both = 2 * height
+    dma = pltpu.SemaphoreType.DMA
+    return pl.pallas_call(
+        functools.partial(decode_kernel, count),
+        out_shape=jax.ShapeDtypeStruct((1, frames, local_rows, columns, channels), jnp.bfloat16),
+        in_specs=[pl.BlockSpec(memory_space=pl.ANY)]
+        + [pl.BlockSpec(memory_space=pltpu.VMEM)] * 3,
+        out_specs=pl.BlockSpec(memory_space=pltpu.VMEM),
+        scratch_shapes=[
+            pltpu.VMEM((frames, height, width, channels), jnp.bfloat16),
+            pltpu.VMEM((frames, height * width, channels), jnp.float32),
+            pltpu.VMEM((2, width, both, channels), jnp.bfloat16),
+            pltpu.VMEM((2, width, both, channels), jnp.bfloat16),
+            pltpu.VMEM((2, 2, width, both, channels), jnp.bfloat16),
+            pltpu.VMEM((2, 2, 2, 2, both, channels), jnp.bfloat16),
+            pltpu.VMEM((2, 2 * count, 8, channels), jnp.float32),
+            pltpu.VMEM((4, 3, width + 2, both, channels), jnp.bfloat16),
+            dma,
+            dma((count,)),
+            dma((count,)),
+            dma((2, 2 * count)),
+            dma((2, 2 * count)),
+            dma((2, 2, 2)),
+            dma((2, 2, 2)),
+            dma((2,)),
+            dma((2,)),
+            dma((count,)),
+            dma((count,)),
+            pltpu.SemaphoreType.REGULAR,
+        ],
+        compiler_params=pltpu.CompilerParams(
+            collective_id=0, has_side_effects=True, vmem_limit_bytes=48 * 2**20
+        ),
+    )(latents, first, second, small)
+
+
 def solution(mesh):
     in_specs = (
         P(None, "tm", "rows", None, None),
@@ -104,4 +535,22 @@
         P("segment", None),
     )
     out_specs = P("segment", "tm", "rows", None, None)
-    return jax.shard_map(body, mesh=mesh, in_specs=in_specs, out_specs=out_specs, check_vma=False)
+    sizes = dict(mesh.shape)
+
+    def run(latents, *params):
+        micro, frames, height, columns, channels = latents.shape
+        count = sizes["rows"]
+        fits = (
+            micro == sizes["segment"]
+            and sizes["tm"] == 2
+            and frames == 8
+            and height % (8 * 1) == 0
+            and columns % (count * ROWS) == 0
+            and channels == 4 * GROUPS
+        )
+        inner = body if fits else plain_body
+        return jax.shard_map(
+            inner, mesh=mesh, in_specs=in_specs, out_specs=out_specs, check_vma=False
+        )(latents, *params)
+
+    return run

time: 297 us -> 194 us (0.65)
  blocking collectives: 88.7 us -> 9.52 us
  Pallas kernels: 0 us -> 74.3 us
  starting transfers between devices: 43 us -> 0.04 us
  matrix products: 26.5 us -> 0 us
  waiting for transfers between devices: 103 us -> 91.5 us
  local copies, waits for them, and re-layouts: 13.6 us -> 3.93 us
  other arithmetic: 7.41 us -> 0.72 us
    psum x8 -> x0, blocking collectives: 80.6 us -> none  [normalize(): lax.psum((jnp.sum(grouped, axis=(0, 1, 2, 4)), jnp.sum(grouped * grouped,...]
    pallas_call x0 -> x1, Pallas kernels: none -> 74.3 us  [body(): pl.pallas_call(functools.partial(decode_kernel, count), out_shape=jax.Sha...]
    ppermute x24 -> x0, waiting for transfers between devices: 67.9 us -> none  [the longest x8 33 us: padded_2(): lax.ppermute(lax.slice_in_dim(block, 0, width, axis=dim), axis, backward)]
    ppermute x24 -> x0, starting transfers between devices: 42.9 us -> none  [the longest x8 21.7 us: padded_2(): lax.ppermute(lax.slice_in_dim(block, block.shape[dim] - width, None, axis...]
    all_gather x1, waiting for transfers between devices: 18.9 us -> 49.1 us  [body(): second = lax.all_gather(conv_second, 'segment', axis=0, tiled=True)]
    conv_general_dilated x8 -> x0, matrix products: 26.5 us -> none  [convolve(): lax.conv_general_dilated(padded[None], kernel, (1, 1, 1), 'VALID', dimens...]
    all_gather x1, waiting for transfers between devices: 14.6 us -> 40.9 us  [body(): first = lax.all_gather(conv_first, 'segment', axis=0, tiled=True)]
  transfers between devices with their start and end apart: 26 -> 2, of which waited for: 26 -> 2; matrix products, arithmetic and copies ran while one was open for 3% -> 0% of each run, Pallas kernels for 0% -> 0%
where the time goes in v1:
time: 194 us; the launch traced here: 193 us
  waiting for transfers between devices  91.5 us (47%)
  Pallas kernels  74.3 us (38%)
  between operations  13.4 us (7%)
  blocking collectives  9.52 us (5%)
  local copies, waits for them, and re-layouts  3.93 us (2%)
    pallas_call x1, Pallas kernels, body(): pl.pallas_call(functools.partial(decode_kernel, count), out_shape=jax.Sha...  74.3 us
    all_gather x1, waiting for transfers between devices, body(): second = lax.all_gather(conv_second, 'segment', axis=0, tiled=True)  49.1 us
    all_gather x1, waiting for transfers between devices, body(): first = lax.all_gather(conv_first, 'segment', axis=0, tiled=True)  40.9 us
    all_gather x1, blocking collectives, body(): lax.all_gather(small, 'segment', axis=0, tiled=True).astype(jnp.float32)  9.52 us
    unnamed x5, local copies, waits for them, and re-layouts  3.93 us
  transfers between devices with their start and end apart: 2, of which 2 were waited for; matrix products, arithmetic and copies ran while one was open for 0% of the time, Pallas kernels for 0%

profile of v1, /device:TPU:0, one launch (start us, length us, event | category | flops | bytes accessed | tf_op | source)
XLA Modules:
  0.0 193.4 jit_solution(11683109820132572648)
XLA Ops:
  6.5 0.0 all-gather.3.cloned.1.call-start
  6.5 0.7 all-gather.3.cloned.1.call-update
  7.3 0.0 all-gather.5.cloned.1.call-start
  7.3 0.7 all-gather.5.cloned.1.call-update
  8.0 0.7 pad_maximum_fusion
  8.7 9.5 %all_gather.11 = bf16[4,4,128]{2,1,0:T(4,128)(2,1)S(1)} all-gather(bf16[1,4,128]{2,1,0:T(4,128)(2,1)S(1)} %pad_maximum_fusion), channel_id=1, replica_groups=mesh['rows'=4,'segment'=4,'tm'=2] {'segment'}, dimensions={0}, use_global_device_ids=true | all-gather | bytes 5120 | tf_op jit(solution)/shard_map/all_gather | solution.py:488
  18.2 40.9 %all-gather.3.cloned.1.call-done.first = bf16[4,3,3,3,128,128]{5,4,3,2,1,0:T(8,128)(2,1)} async-done(((bf16[1,3,3,3,128,128]{5,4,3,2,1,0:T(8,128)(2,1)}), bf16[4,3,3,3,128,128]{5,4,3,2,1,0:T(8,128)(2,1)}) %all-gather.3.cloned.1.call-update) | async-done | bytes 3538960 | tf_op jit(solution)/shard_map/all_gather | solution.py:489
  59.2 49.1 %all-gather.5.cloned.1.call-done.second = bf16[4,3,3,3,128,128]{5,4,3,2,1,0:T(8,128)(2,1)} async-done(((bf16[1,3,3,3,128,128]{5,4,3,2,1,0:T(8,128)(2,1)}), bf16[4,3,3,3,128,128]{5,4,3,2,1,0:T(8,128)(2,1)}) %all-gather.5.cloned.1.call-update) | async-done | bytes 3538960 | tf_op jit(solution)/shard_map/all_gather | solution.py:490
  108.3 0.0 copy-start
  108.3 2.0 %copy-done = bf16[4,3,3,3,128,128]{5,4,3,2,1,0:T(8,128)(2,1)S(1)} copy-done((bf16[4,3,3,3,128,128]{5,4,3,2,1,0:T(8,128)(2,1)S(1)}, bf16[4,3,3,3,128,128]{5,4,3,2,1,0:T(8,128)(2,1)}, u32[]{:S(2)}) %copy-start) | copy-done | bytes 3538968
  110.3 0.0 copy-start.1
  110.3 1.2 copy-done.1
  111.5 74.3 %shard_map.73 = bf16[1,4,2,128,128]{4,3,2,1,0:T(8,128)(2,1)S(1)} custom-call(bf16[4,4,2,128,128]{4,3,2,1,0:T(8,128)(2,1)S(1)} %copy-done.1, bf16[4,3,3,3,128,128]{5,4,3,2,1,0:T(8,128)(2,1)S(1)} %copy-done, bf16[4,3,3,3,128,128]{5,4,3,2,1,0:T(8,128)(2,1)} %all-gather.5.cloned.1.call-done.second, f32[4,4,128]{2,1,0:T(4,128)S(1)} %convert_element_type.3.small), custom_call_target="tpu_custom_call" | custom-call | tf_op jit(solution)/shard_map/pallas_call | solution.py:493
  185.8 0.7 copy.9
  (1 shorter events, 0.0 us)
Async XLA Ops:
  6.5 52.7 %all-gather.3.cloned.1.call-start = ((), (), s32[]{:S(2)}) async-start(), calls=%async_computation | async-start | bytes 4423680 | tf_op jit(solution)/shard_map/all_gather | solution.py:489
  7.3 101.1 %all-gather.5.cloned.1.call-start = ((), (), s32[]{:S(2)}) async-start(), calls=%async_computation.1 | async-start | bytes 4423680 | tf_op jit(solution)/shard_map/all_gather | solution.py:490
  108.3 2.0 %copy-start = (bf16[4,3,3,3,128,128]{5,4,3,2,1,0:T(8,128)(2,1)S(1)}, bf16[4,3,3,3,128,128]{5,4,3,2,1,0:T(8,128)(2,1)}, u32[]{:S(2)}) copy-start(bf16[4,3,3,3,128,128]{5,4,3,2,1,0:T(8,128)(2,1)} %all-gather.3.cloned.1.call-done.first) | copy-start | bytes 10616836
  110.3 1.2 copy-start.1
Sparse Core Ops, SparseCore 0:
  9.2 49.9 all-gather.2
  61.0 47.2 all-gather.4

commit v2 on v1

--- a/solution.py
+++ b/solution.py
@@ -123,7 +123,10 @@
     latents,
     first,
     second,
-    small,
+    gain_first,
+    bias_first,
+    gain_second,
+    bias_second,
     out,
     staged,
     turned,
@@ -145,6 +148,15 @@
     out_send,
     out_recv,
     free_sem,
+    kernels,
+    small,
+    param_send,
+    param_recv,
+    load_sem,
+    w_send,
+    w_recv,
+    half_send,
+    half_recv,
 ):
     frames, height, width, channels = staged.shape
     local_rows = height // count
@@ -163,7 +175,145 @@
         if k:
             pl.semaphore_signal(barrier, inc=1, device_id=at(other, span), device_id_type=MESH)
         pl.semaphore_signal(barrier, inc=1, device_id=at(other, 1 - span), device_id_type=MESH)
-    pl.semaphore_wait(barrier, 2 * count - 1)
+    for k in range(1, 4):
+        pl.semaphore_signal(
+            barrier, inc=1, device_id={"segment": segment ^ k}, device_id_type=MESH
+        )
+    pl.semaphore_wait(barrier, 2 * count + 2)
+
+    given = (first, second)
+    layers = kernels.shape[0] // 2
+    depth = channels // 2
+
+    def tensor_part(ref, half, chunk, chunks):
+        rows = pl.ds(pl.multiple_of(half * depth, depth), depth)
+        size = 3 // chunks
+        return ref.at[pl.ds(chunk * size, size), :, :, rows]
+
+    def chunks_of(j):
+        return 3 if j < 2 else 1
+
+    def remote_half(j, chunk, source, to, slot):
+        return pltpu.make_async_remote_copy(
+            src_ref=tensor_part(source, span, chunk, chunks_of(j)),
+            dst_ref=tensor_part(kernels.at[j], span, chunk, chunks_of(j)),
+            send_sem=w_send.at[j, slot, chunk],
+            recv_sem=w_recv.at[j, chunk],
+            device_id={"segment": to},
+            device_id_type=MESH,
+        )
+
+    def core_half(j, chunk, half):
+        return pltpu.make_async_remote_copy(
+            src_ref=tensor_part(kernels.at[j], half, chunk, chunks_of(j)),
+            dst_ref=tensor_part(kernels.at[j], half, chunk, chunks_of(j)),
+            send_sem=half_send.at[j, chunk],
+            recv_sem=half_recv.at[j, chunk],
+            device_id={"tm": 1 - span},
+            device_id_type=MESH,
+        )
+
+    def move(name):
+        kind, j = name[0], int(name[1])
+        away = segment ^ (j // 2)
+        source = given[j % 2].at[0]
+        first_to = segment ^ (1 + span)
+        second_to = segment ^ (2 - span)
+        passes = away == 1 + span
+        each = range(chunks_of(j))
+        if kind == "P":
+
+            @pl.when(away == 0)
+            def _():
+                for c in each:
+                    remote_half(j, c, source, first_to, 0).start()
+
+        if kind == "S":
+
+            @pl.when(away == 0)
+            def _():
+                for c in each:
+                    remote_half(j, c, source, first_to, 0).wait_send()
+                for c in each:
+                    remote_half(j, c, source, second_to, 1).start()
+
+        if kind == "F":
+
+            @pl.when(passes)
+            def _():
+                for c in each:
+                    remote_half(j, c, kernels.at[j], second_to, 0).wait_recv()
+                    remote_half(j, c, kernels.at[j], second_to, 0).start()
+                    core_half(j, c, span).start()
+
+        if kind == "R":
+
+            @pl.when((away > 0) & jnp.logical_not(passes))
+            def _():
+                for c in each:
+                    remote_half(j, c, kernels.at[j], second_to, 0).wait_recv()
+                    core_half(j, c, span).start()
+
+        if kind == "G":
+
+            @pl.when(away > 0)
+            def _():
+                for c in each:
+                    core_half(j, c, 1 - span).wait_recv()
+
+            @pl.when(away == 0)
+            def _():
+                pltpu.make_async_copy(source, kernels.at[j], load_sem.at[j]).wait()
+
+        if kind == "W":
+
+            @pl.when(away == 0)
+            def _():
+                for c in each:
+                    remote_half(j, c, source, second_to, 1).wait_send()
+
+            @pl.when(passes)
+            def _():
+                for c in each:
+                    remote_half(j, c, kernels.at[j], second_to, 0).wait_send()
+
+            @pl.when(away > 0)
+            def _():
+                for c in each:
+                    core_half(j, c, span).wait_send()
+
+    plan = {
+        "start": ("P0", "P2", "P4", "P6",),
+        "early": ("F0", "S0",),
+        "a0": ("R0", "P1", "S2", "S4", "S6",),
+        "b0": ("S1", "G0",),
+        "a1": ("F1", "P7",),
+        "b1": ("F2", "P3", "P5", "R1", "G1",),
+        "a2": ("S3", "S5", "S7", "F4",),
+        "b2": ("R2", "F3", "G2",),
+        "a3": ("F5", "F6",),
+        "b3": ("R3", "R4", "G3",),
+        "a4": ("F7",),
+        "b4": ("R5", "R6", "G4",),
+        "a5": ("R7",),
+        "b5": ("G5",),
+        "b6": ("G6",),
+        "b7": ("G7",),
+        "end": ("W0", "W1", "W2", "W3", "W4", "W5", "W6", "W7",),
+    }
+
+    def moves(point):
+        for name in plan.get(point, ()):
+            move(name)
+
+    def moves_at(letter, which, layer):
+        for known in range(layers):
+            point = letter + str(2 * known + which)
+            if point in plan:
+
+                @pl.when(layer == known)
+                def _(point=point):
+                    moves(point)
 
     def incoming(k, me, to):
         return pltpu.make_async_remote_copy(
@@ -175,14 +325,40 @@
             device_id_type=MESH,
         )
 
+    moves("start")
     for k in range(1, count):
         incoming(k, row, lax.rem(row + k, count)).start()
+    for j in range(2 * layers):
+
+        @pl.when(segment == j // 2)
+        def _(j=j):
+            pltpu.make_async_copy(given[j % 2].at[0], kernels.at[j], load_sem.at[j]).start()
+
+    index = lax.broadcasted_iota(jnp.int32, (8, channels), 0)
+    packed = jnp.zeros((8, channels), jnp.float32)
+    for k, ref in enumerate((gain_first, bias_first, gain_second, bias_second)):
+        packed = jnp.where(index == k, ref[...].astype(jnp.float32), packed)
+    small[segment] = packed
+
+    def param_copy(k, me):
+        return pltpu.make_async_remote_copy(
+            src_ref=small.at[me],
+            dst_ref=small.at[me],
+            send_sem=param_send.at[k],
+            recv_sem=param_recv.at[me],
+            device_id={"segment": segment ^ k},
+            device_id_type=MESH,
+        )
+
+    for k in range(1, 4):
+        param_copy(k, segment).start()
     own = pltpu.make_async_copy(
         latents.at[segment, :, :, pl.ds(pl.multiple_of(row * width, width), width)],
         staged.at[:, pl.ds(row * local_rows, local_rows)],
         own_sem,
     )
     own.start()
+    moves("early")
     own.wait()
     for k in range(1, count):
         other = lax.rem(row + k, count)
@@ -421,22 +597,27 @@
         def _():
             pl.semaphore_wait(free_sem, 1)
 
-    layers = first.shape[0]
     exchange(0, values, partial)
+    for k in range(1, 4):
+        param_copy(k, segment ^ k).wait_recv()
 
     @pl.loop(0, layers)
     def _(layer):
+        moves_at("a", 0, layer)
         receive(0, values)
         give(layer > 0)
         activate(0, values, small[layer, 0:1], small[layer, 1:2])
-        partial = convolution(first.at[layer], store_hidden)
+        moves_at("b", 0, layer)
+        partial = convolution(kernels.at[2 * layer], store_hidden)
         finish_sends(0, values)
         take(layer > 0)
         exchange(1, hidden, partial)
+        moves_at("a", 1, layer)
         receive(1, hidden)
         give(layer < layers - 1)
         activate(1, hidden, small[layer, 2:3], small[layer, 3:4])
-        partial = convolution(second.at[layer], store_values)
+        moves_at("b", 1, layer)
+        partial = convolution(kernels.at[2 * layer + 1], store_values)
         finish_sends(1, hidden)
 
         @pl.when(layer < layers - 1)
@@ -473,6 +654,9 @@
     )
     own.start()
     own.wait()
+    moves("end")
+    for k in range(1, 4):
+        param_copy(k, segment).wait_send()
     for k in range(1, count):
         other = lax.rem(row + k, count)
         outgoing(k, other, row).wait_recv()
@@ -484,17 +668,13 @@
     count = lax.axis_size("rows")
     width = columns // count
     height = local_rows * count
-    small = jnp.stack([gain_first, bias_first, gain_second, bias_second], axis=1)
-    small = lax.all_gather(small, "segment", axis=0, tiled=True).astype(jnp.float32)
-    first = lax.all_gather(conv_first, "segment", axis=0, tiled=True)
-    second = lax.all_gather(conv_second, "segment", axis=0, tiled=True)
     both = 2 * height
     dma = pltpu.SemaphoreType.DMA
     return pl.pallas_call(
         functools.partial(decode_kernel, count),
         out_shape=jax.ShapeDtypeStruct((1, frames, local_rows, columns, channels), jnp.bfloat16),
-        in_specs=[pl.BlockSpec(memory_space=pl.ANY)]
-        + [pl.BlockSpec(memory_space=pltpu.VMEM)] * 3,
+        in_specs=[pl.BlockSpec(memory_space=pl.ANY)] * 3
+        + [pl.BlockSpec(memory_space=pltpu.VMEM)] * 4,
         out_specs=pl.BlockSpec(memory_space=pltpu.VMEM),
         scratch_shapes=[
             pltpu.VMEM((frames, height, width, channels), jnp.bfloat16),
@@ -517,11 +697,20 @@
             dma((count,)),
             dma((count,)),
             pltpu.SemaphoreType.REGULAR,
+            pltpu.VMEM((8,) + conv_first.shape[1:], jnp.bfloat16),
+            pltpu.VMEM((4, 8, channels), jnp.float32),
+            dma((4,)),
+            dma((4,)),
+            dma((8,)),
+            dma((8, 2, 3)),
+            dma((8, 3)),
+            dma((8, 3)),
+            dma((8, 3)),
         ],
         compiler_params=pltpu.CompilerParams(
             collective_id=0, has_side_effects=True, vmem_limit_bytes=48 * 2**20
         ),
-    )(latents, first, second, small)
+    )(latents, conv_first, conv_second, gain_first, bias_first, gain_second, bias_second)
 
 
 def solution(mesh):
@@ -541,7 +730,9 @@
         micro, frames, height, columns, channels = latents.shape
         count = sizes["rows"]
         fits = (
-            micro == sizes["segment"]
+            micro == sizes["segment"] == 4
+            and params[0].shape == (4, 3, 3, 3, channels, channels)
+            and count < 8
             and sizes["tm"] == 2
             and frames == 8
             and height % (8 * 1) == 0

time: 194 us -> 95.4 us (0.49)
  waiting for transfers between devices: 91.5 us -> 0 us
  between operations: 13.4 us -> 0.02 us
  Pallas kernels: 74.3 us -> 87 us
  blocking collectives: 9.52 us -> 0 us
  local copies, waits for them, and re-layouts: 3.93 us -> 6.88 us
    all_gather x2 -> x0, waiting for transfers between devices: 90.1 us -> none  [the longest x1 49.1 us: body(): second = lax.all_gather(conv_second, 'segment', axis=0, tiled=True)]
    pallas_call x1, Pallas kernels: 74.3 us -> 87 us  [body(): pl.pallas_call(functools.partial(decode_kernel, count), out_shape=jax.Sha...]
    all_gather x1 -> x0, blocking collectives: 9.52 us -> none  [body(): lax.all_gather(small, 'segment', axis=0, tiled=True).astype(jnp.float32)]
    unnamed x5 -> x15, local copies, waits for them, and re-layouts: 3.93 us -> 6.88 us
  transfers between devices with their start and end apart: 2 -> 0, of which waited for: 2 -> 0; matrix products, arithmetic and copies ran while one was open for 0% -> 0% of each run, Pallas kernels for 0% -> 0%
where the time goes in v2:
time: 95.4 us; the launch traced here: 93.9 us
  Pallas kernels  87 us (91%)
  local copies, waits for them, and re-layouts  6.88 us (7%)
    pallas_call x1, Pallas kernels, body(): pl.pallas_call(functools.partial(decode_kernel, count), out_shape=jax.Sha...  87 us
    unnamed x15, local copies, waits for them, and re-layouts  6.88 us

profile of v2, /device:TPU:0, one launch (start us, length us, event | category | flops | bytes accessed | tf_op | source)
XLA Modules:
  0.0 93.9 jit_solution(4300237126091767478)
XLA Ops:
  0.0 0.0 copy-start
  0.0 1.2 %copy-done = bf16[4,4,2,128,128]{4,3,2,1,0:T(8,128)(2,1)S(1)} copy-done((bf16[4,4,2,128,128]{4,3,2,1,0:T(8,128)(2,1)S(1)}, bf16[4,4,2,128,128]{4,3,2,1,0:T(8,128)(2,1)}, u32[]{:S(2)}) %copy-start) | copy-done | bytes 1048600
  1.2 0.0 copy-start.1
  1.2 1.2 %copy-done.1 = bf16[1,3,3,3,128,128]{5,4,3,2,1,0:T(8,128)(2,1)S(1)} copy-done((bf16[1,3,3,3,128,128]{5,4,3,2,1,0:T(8,128)(2,1)S(1)}, bf16[1,3,3,3,128,128]{5,4,3,2,1,0:T(8,128)(2,1)}, u32[]{:S(2)}) %copy-start.1) | copy-done | bytes 884760
  2.4 0.0 copy-start.2
  2.4 1.2 %copy-done.2 = bf16[1,3,3,3,128,128]{5,4,3,2,1,0:T(8,128)(2,1)S(1)} copy-done((bf16[1,3,3,3,128,128]{5,4,3,2,1,0:T(8,128)(2,1)S(1)}, bf16[1,3,3,3,128,128]{5,4,3,2,1,0:T(8,128)(2,1)}, u32[]{:S(2)}) %copy-start.2) | copy-done | bytes 884760
  3.6 0.0 copy-start.3
  3.6 0.7 copy-done.3
  4.2 0.0 copy-start.4
  4.2 0.7 copy-done.4
  4.9 0.0 copy-start.5
  4.9 0.7 copy-done.5
  5.5 0.0 copy-start.6
  5.5 0.7 copy-done.6
  6.2 87.0 %shard_map.73 = bf16[1,4,2,128,128]{4,3,2,1,0:T(8,128)(2,1)S(1)} custom-call(bf16[4,4,2,128,128]{4,3,2,1,0:T(8,128)(2,1)S(1)} %copy-done, bf16[1,3,3,3,128,128]{5,4,3,2,1,0:T(8,128)(2,1)S(1)} %copy-done.1, bf16[1,3,3,3,128,128]{5,4,3,2,1,0:T(8,128)(2,1)S(1)} %copy-done.2, bf16[1,128]{1,0:T(2,128)(2,1)S(1)} %copy-done.3, bf16[1,128]{1,0:T(2,128)(2,1)S(1)} %copy-done.4, ...), custom_call_target="tpu_custom_call" | custom-call | tf_op jit(solution)/shard_map/pallas_call | solution.py:673
  93.2 0.7 copy.9
Async XLA Ops:
  0.0 1.2 %copy-start = (bf16[4,4,2,128,128]{4,3,2,1,0:T(8,128)(2,1)S(1)}, bf16[4,4,2,128,128]{4,3,2,1,0:T(8,128)(2,1)}, u32[]{:S(2)}) copy-start(bf16[4,4,2,128,128]{4,3,2,1,0:T(8,128)(2,1)} %latents.1) | copy-start | bytes 3145732
  1.2 1.2 %copy-start.1 = (bf16[1,3,3,3,128,128]{5,4,3,2,1,0:T(8,128)(2,1)S(1)}, bf16[1,3,3,3,128,128]{5,4,3,2,1,0:T(8,128)(2,1)}, u32[]{:S(2)}) copy-start(bf16[1,3,3,3,128,128]{5,4,3,2,1,0:T(8,128)(2,1)} %first.1) | copy-start | bytes 2654212
  2.4 1.2 %copy-start.2 = (bf16[1,3,3,3,128,128]{5,4,3,2,1,0:T(8,128)(2,1)S(1)}, bf16[1,3,3,3,128,128]{5,4,3,2,1,0:T(8,128)(2,1)}, u32[]{:S(2)}) copy-start(bf16[1,3,3,3,128,128]{5,4,3,2,1,0:T(8,128)(2,1)} %second.1) | copy-start | bytes 2654212
  3.6 0.7 copy-start.3
  4.2 0.7 copy-start.4
  4.9 0.7 copy-start.5
  5.5 0.7 copy-start.6

commit v3 on v2

--- a/solution.py
+++ b/solution.py
@@ -157,6 +157,8 @@
     w_recv,
     half_send,
     half_recv,
+    raw_params,
+    raw_sem,
 ):
     frames, height, width, channels = staged.shape
     local_rows = height // count
@@ -233,8 +235,8 @@
             @pl.when(away == 0)
             def _():
                 for c in each:
-                    remote_half(j, c, source, first_to, 0).wait_send()
-                for c in each:
+                    if j == 0:
+                        remote_half(j, c, source, first_to, 0).wait_send()
                     remote_half(j, c, source, second_to, 1).start()
 
         if kind == "F":
@@ -270,6 +272,8 @@
             @pl.when(away == 0)
             def _():
                 for c in each:
+                    if j > 0:
+                        remote_half(j, c, source, first_to, 0).wait_send()
                     remote_half(j, c, source, second_to, 1).wait_send()
 
             @pl.when(passes)
@@ -283,23 +287,25 @@
                     core_half(j, c, span).wait_send()
 
     plan = {
-        "start": ("P0", "P2", "P4", "P6",),
-        "early": ("F0", "S0",),
-        "a0": ("R0", "P1", "S2", "S4", "S6",),
-        "b0": ("S1", "G0",),
-        "a1": ("F1", "P7",),
-        "b1": ("F2", "P3", "P5", "R1", "G1",),
-        "a2": ("S3", "S5", "S7", "F4",),
-        "b2": ("R2", "F3", "G2",),
-        "a3": ("F5", "F6",),
-        "b3": ("R3", "R4", "G3",),
+        "start": ("P0", "P2", "P4", "P6"),
+        "early": ("F0", "S0"),
+        "mid": ("P1",),
+        "a0": ("R0", "S2", "S4", "S6"),
+        "b0": ("S1", "G0"),
+        "a1": ("F1",),
+        "r1": ("F2",),
+        "b1": ("P3", "P5", "R1", "G1"),
+        "a2": ("F3", "S3", "S5", "F4"),
+        "b2": ("P7", "R2", "G2"),
+        "a3": ("F5", "F6"),
+        "b3": ("S7", "R3", "R4", "G3"),
         "a4": ("F7",),
-        "b4": ("R5", "R6", "G4",),
+        "b4": ("R5", "R6", "G4"),
         "a5": ("R7",),
         "b5": ("G5",),
         "b6": ("G6",),
         "b7": ("G7",),
-        "end": ("W0", "W1", "W2", "W3", "W4", "W5", "W6", "W7",),
+        "end": ("W0", "W1", "W2", "W3", "W4", "W5", "W6", "W7"),
     }
 
     def moves(point):
@@ -335,9 +341,17 @@
             pltpu.make_async_copy(given[j % 2].at[0], kernels.at[j], load_sem.at[j]).start()
 
     index = lax.broadcasted_iota(jnp.int32, (8, channels), 0)
+    raw = [
+        pltpu.make_async_copy(ref, raw_params.at[k], raw_sem.at[k])
+        for k, ref in enumerate((gain_first, bias_first, gain_second, bias_second))
+    ]
+    for copy in raw:
+        copy.start()
+    for copy in raw:
+        copy.wait()
     packed = jnp.zeros((8, channels), jnp.float32)
-    for k, ref in enumerate((gain_first, bias_first, gain_second, bias_second)):
-        packed = jnp.where(index == k, ref[...].astype(jnp.float32), packed)
+    for k in range(4):
+        packed = jnp.where(index == k, raw_params[k].astype(jnp.float32), packed)
     small[segment] = packed
 
     def param_copy(k, me):
@@ -363,6 +377,7 @@
     for k in range(1, count):
         other = lax.rem(row + k, count)
         incoming(k, other, row).wait_recv()
+    moves("mid")
 
     for f in range(frames):
         turned[f] = staged[f].astype(jnp.float32).reshape(height * width, channels)
@@ -539,7 +554,7 @@
                 )
 
     def convolution(weights, store):
-        step = width
+        step = width // 2
         partial = None
         for x in range(0, width, step):
             left, right = [], []
@@ -605,6 +620,7 @@
     def _(layer):
         moves_at("a", 0, layer)
         receive(0, values)
+        moves_at("r", 0, layer)
         give(layer > 0)
         activate(0, values, small[layer, 0:1], small[layer, 1:2])
         moves_at("b", 0, layer)
@@ -614,6 +630,7 @@
         exchange(1, hidden, partial)
         moves_at("a", 1, layer)
         receive(1, hidden)
+        moves_at("r", 1, layer)
         give(layer < layers - 1)
         activate(1, hidden, small[layer, 2:3], small[layer, 3:4])
         moves_at("b", 1, layer)
@@ -673,8 +690,7 @@
     return pl.pallas_call(
         functools.partial(decode_kernel, count),
         out_shape=jax.ShapeDtypeStruct((1, frames, local_rows, columns, channels), jnp.bfloat16),
-        in_specs=[pl.BlockSpec(memory_space=pl.ANY)] * 3
-        + [pl.BlockSpec(memory_space=pltpu.VMEM)] * 4,
+        in_specs=[pl.BlockSpec(memory_space=pltpu.HBM)] * 7,
         out_specs=pl.BlockSpec(memory_space=pltpu.VMEM),
         scratch_shapes=[
             pltpu.VMEM((frames, height, width, channels), jnp.bfloat16),
@@ -706,9 +722,11 @@
             dma((8, 3)),
             dma((8, 3)),
             dma((8, 3)),
+            pltpu.VMEM((4, 1, channels), jnp.bfloat16),
+            dma((4,)),
         ],
         compiler_params=pltpu.CompilerParams(
-            collective_id=0, has_side_effects=True, vmem_limit_bytes=48 * 2**20
+            collective_id=0, has_side_effects=True, vmem_limit_bytes=64 * 2**20 - 2**17
         ),
     )(latents, conv_first, conv_second, gain_first, bias_first, gain_second, bias_second)
 

time: 95.4 us -> 81.8 us (0.86); the launches traced: 93.9 us -> 81.6 us
  Pallas kernels: 87 us -> 80 us
  local copies, waits for them, and re-layouts: 6.88 us -> 1.67 us
    pallas_call x1, Pallas kernels: 87 us -> 80 us  [body(): pl.pallas_call(functools.partial(decode_kernel, count), out_shape=jax.Sha...]
    unnamed x15 -> x1, local copies, waits for them, and re-layouts: 6.88 us -> 1.67 us
where the time goes in v3:
time: 81.8 us; the launch traced here: 81.6 us
  Pallas kernels  80 us (98%)
  local copies, waits for them, and re-layouts  1.67 us (2%)
    pallas_call x1, Pallas kernels, body(): pl.pallas_call(functools.partial(decode_kernel, count), out_shape=jax.Sha...  80 us
    unnamed x1, local copies, waits for them, and re-layouts  1.67 us

profile of v3, /device:TPU:0, one launch (start us, length us, event | category | flops | bytes accessed | tf_op | source)
XLA Modules:
  0.0 81.6 jit_solution(16969477811214991236)
XLA Ops:
  0.0 80.0 %shard_map.73 = bf16[1,4,2,128,128]{4,3,2,1,0:T(8,128)(2,1)} custom-call(bf16[4,4,2,128,128]{4,3,2,1,0:T(8,128)(2,1)} %latents.1, bf16[1,3,3,3,128,128]{5,4,3,2,1,0:T(8,128)(2,1)} %first.1, bf16[1,3,3,3,128,128]{5,4,3,2,1,0:T(8,128)(2,1)} %second.1, bf16[1,128]{1,0:T(2,128)(2,1)} %gain_first.1, bf16[1,128]{1,0:T(2,128)(2,1)} %bias_first.1, ...), custom_call_target="tpu_custom_call" | custom-call | tf_op jit(solution)/shard_map/pallas_call | solution.py:690
  80.0 1.7 %copy.9 = bf16[1,4,2,128,128]{4,3,2,1,0:T(8,128)(2,1)} copy(bf16[1,4,2,128,128]{4,3,2,1,0:T(8,128)(2,1)} %shard_map.73) | data formatting | bytes 524288

commit v4 on v3

--- a/solution.py
+++ b/solution.py
@@ -201,7 +201,7 @@
             dst_ref=tensor_part(kernels.at[j], span, chunk, chunks_of(j)),
             send_sem=w_send.at[j, slot, chunk],
             recv_sem=w_recv.at[j, chunk],
-            device_id={"segment": to},
+            device_id={"rows": row ^ 1} if to is None else {"segment": to},
             device_id_type=MESH,
         )
 
@@ -215,14 +215,24 @@
             device_id_type=MESH,
         )
 
+    routes = "ZZVXVVVV"
+
     def move(name):
         kind, j = name[0], int(name[1])
+        route = routes[j]
         away = segment ^ (j // 2)
         source = given[j % 2].at[0]
-        first_to = segment ^ (1 + span)
-        second_to = segment ^ (2 - span)
-        passes = away == 1 + span
         each = range(chunks_of(j))
+        if route == "X":
+            first_to = segment ^ 1
+            second_to = pass_to = segment ^ 2
+            passes = away == 1
+        else:
+            turn = lax.rem(row + span, 2) if route == "Z" else span
+            first_to = segment ^ (1 + turn)
+            second_to = pass_to = segment ^ (2 - turn)
+            passes = away == 1 + turn
+        here = kernels.at[j]
         if kind == "P":
 
             @pl.when(away == 0)
@@ -230,13 +240,19 @@
                 for c in each:
                     remote_half(j, c, source, first_to, 0).start()
 
+        if kind == "Q":
+
+            @pl.when(away == 0)
+            def _():
+                for c in each:
+                    remote_half(j - 1, c, given[(j - 1) % 2].at[0], first_to, 0).wait_send()
+                    remote_half(j, c, source, first_to, 0).start()
+
         if kind == "S":
 
             @pl.when(away == 0)
             def _():
                 for c in each:
-                    if j == 0:
-                        remote_half(j, c, source, first_to, 0).wait_send()
                     remote_half(j, c, source, second_to, 1).start()
 
         if kind == "F":
@@ -244,8 +260,10 @@
             @pl.when(passes)
             def _():
                 for c in each:
-                    remote_half(j, c, kernels.at[j], second_to, 0).wait_recv()
-                    remote_half(j, c, kernels.at[j], second_to, 0).start()
+                    remote_half(j, c, here, pass_to, 0).wait_recv()
+                    remote_half(j, c, here, pass_to, 0).start()
+                    if route == "Z":
+                        remote_half(j, c, here, None, 1).start()
                     core_half(j, c, span).start()
 
         if kind == "R":
@@ -253,7 +271,7 @@
             @pl.when((away > 0) & jnp.logical_not(passes))
             def _():
                 for c in each:
-                    remote_half(j, c, kernels.at[j], second_to, 0).wait_recv()
+                    remote_half(j, c, here, pass_to, 0).wait_recv()
                     core_half(j, c, span).start()
 
         if kind == "G":
@@ -274,12 +292,15 @@
                 for c in each:
                     if j > 0:
                         remote_half(j, c, source, first_to, 0).wait_send()
-                    remote_half(j, c, source, second_to, 1).wait_send()
+                    if route != "Z":
+                        remote_half(j, c, source, second_to, 1).wait_send()
 
             @pl.when(passes)
             def _():
                 for c in each:
-                    remote_half(j, c, kernels.at[j], second_to, 0).wait_send()
+                    remote_half(j, c, here, pass_to, 0).wait_send()
+                    if route == "Z":
+                        remote_half(j, c, here, None, 1).wait_send()
 
             @pl.when(away > 0)
             def _():
@@ -288,21 +309,22 @@
 
     plan = {
         "start": ("P0", "P2", "P4", "P6"),
-        "early": ("F0", "S0"),
-        "mid": ("P1",),
-        "a0": ("R0", "S2", "S4", "S6"),
-        "b0": ("S1", "G0"),
-        "a1": ("F1",),
-        "r1": ("F2",),
-        "b1": ("P3", "P5", "R1", "G1"),
-        "a2": ("F3", "S3", "S5", "F4"),
-        "b2": ("P7", "R2", "G2"),
-        "a3": ("F5", "F6"),
-        "b3": ("S7", "R3", "R4", "G3"),
-        "a4": ("F7",),
-        "b4": ("R5", "R6", "G4"),
-        "a5": ("R7",),
+        "early": ("Q1", "F0"),
+        "a0": ("P3", "F1", "R0"),
+        "r0": ("F2", "S2", "S4"),
+        "b0": ("G0",),
+        "a1": ("S3", "S6", "F4", "R1"),
+        "b1": ("G1",),
+        "a2": ("F3", "P5", "R2", "F6"),
+        "b2": ("G2",),
+        "a3": ("S5", "P7", "R4", "R3"),
+        "r3": ("F5",),
+        "b3": ("G3",),
+        "a4": ("S7", "R6"),
+        "b4": ("G4",),
+        "a5": ("F7", "R5"),
         "b5": ("G5",),
+        "r6": ("R7",),
         "b6": ("G6",),
         "b7": ("G7",),
         "end": ("W0", "W1", "W2", "W3", "W4", "W5", "W6", "W7"),
@@ -377,7 +399,6 @@
     for k in range(1, count):
         other = lax.rem(row + k, count)
         incoming(k, other, row).wait_recv()
-    moves("mid")
 
     for f in range(frames):
         turned[f] = staged[f].astype(jnp.float32).reshape(height * width, channels)
@@ -750,7 +771,7 @@
         fits = (
             micro == sizes["segment"] == 4
             and params[0].shape == (4, 3, 3, 3, channels, channels)
-            and count < 8
+            and count % 2 == 0
             and sizes["tm"] == 2
             and frames == 8
             and height % (8 * 1) == 0

time: 81.8 us -> 71.5 us (0.87)
  Pallas kernels: 80 us -> 69.6 us
    pallas_call x1, Pallas kernels: 80 us -> 69.6 us  [body(): pl.pallas_call(functools.partial(decode_kernel, count), out_shape=jax.Sha...]
where the time goes in v4:
time: 71.5 us; the launch traced here: 71.3 us
  Pallas kernels  69.6 us (97%)
  local copies, waits for them, and re-layouts  1.67 us (2%)
    pallas_call x1, Pallas kernels, body(): pl.pallas_call(functools.partial(decode_kernel, count), out_shape=jax.Sha...  69.6 us
    unnamed x1, local copies, waits for them, and re-layouts  1.67 us

profile of v4, /device:TPU:0, one launch (start us, length us, event | category | flops | bytes accessed | tf_op | source)
XLA Modules:
  0.0 71.3 jit_solution(11005273327300772472)
XLA Ops:
  0.0 69.6 %shard_map.73 = bf16[1,4,2,128,128]{4,3,2,1,0:T(8,128)(2,1)} custom-call(bf16[4,4,2,128,128]{4,3,2,1,0:T(8,128)(2,1)} %latents.1, bf16[1,3,3,3,128,128]{5,4,3,2,1,0:T(8,128)(2,1)} %first.1, bf16[1,3,3,3,128,128]{5,4,3,2,1,0:T(8,128)(2,1)} %second.1, bf16[1,128]{1,0:T(2,128)(2,1)} %gain_first.1, bf16[1,128]{1,0:T(2,128)(2,1)} %bias_first.1, ...), custom_call_target="tpu_custom_call" | custom-call | tf_op jit(solution)/shard_map/pallas_call | solution.py:711
  69.6 1.7 %copy.9 = bf16[1,4,2,128,128]{4,3,2,1,0:T(8,128)(2,1)} copy(bf16[1,4,2,128,128]{4,3,2,1,0:T(8,128)(2,1)} %shard_map.73) | data formatting | bytes 524288

commit v5 on v4

--- a/solution.py
+++ b/solution.py
@@ -99,6 +99,8 @@
 
 MESH = pl.DeviceIdType.MESH
 ROWS = 16
+STEPS = 4
+PIECES = 4
 
 
 def group_sums(values):
@@ -516,7 +518,7 @@
         average = total[0:1]
         return average, lax.rsqrt(total[1:2] - average * average + EPS) * gain
 
-    def activate(par, source, gain, bias):
+    def layer_half(par, source, gain, bias, weights, store):
         mine = moments(par, span * count, gain)
         before = moments(par, 0, gain)
         later = span > 0
@@ -533,7 +535,7 @@
                 return jnp.where(index == height - 1, 0.0, pltpu.roll(a, height - 1, 1))
             return a
 
-        def put(q, where, size, tile, older, valid):
+        def put(q, x, size, tile, older, valid):
             a = silu(tile.astype(jnp.float32), mine).reshape(2 * size, height, channels)
             b = silu(older.astype(jnp.float32)[:, height:], before)
             b = jnp.where(later, b, 0.0)
@@ -543,41 +545,30 @@
             for dy in range(3):
                 now = shifted(a, dy).reshape(size, both, channels)
                 old = shifted(b, dy)
-                active[2 + q, dy, where] = now.astype(jnp.bfloat16)
-                active[q, dy, where] = jnp.concatenate([old, now[:, :height]], axis=1).astype(
-                    jnp.bfloat16
+                active[2 + q, dy, x : x + size] = now.astype(jnp.bfloat16)
+                active[q, dy, x : x + size] = jnp.concatenate(
+                    [old, now[:, :height]], axis=1
+                ).astype(jnp.bfloat16)
+
+        def columns_at(x, size):
+            for q in range(2):
+                put(
+                    q, x + 1, size, source[q, x : x + size], sibling[par, q, x : x + size], None
                 )
 
-        step = min(8, width)
-
-        @pl.loop(0, width // step)
-        def _(i):
-            x = i * step
+        def border(side):
+            there = row > 0 if side == 0 else row < count - 1
             for q in range(2):
                 put(
                     q,
-                    pl.ds(x + 1, step),
-                    step,
-                    source[q, pl.ds(x, step)],
-                    sibling[par, q, pl.ds(x, step)],
-                    None,
-                )
-
-        for side, there in ((0, row > 0), (1, row < count - 1)):
-            for q in range(2):
-                put(
-                    q,
-                    pl.ds(0 if side == 0 else width + 1, 1),
+                    0 if side == 0 else width + 1,
                     1,
                     edges[par, side, span, q][None],
                     edges[par, side, 0, q][None],
                     there,
                 )
 
-    def convolution(weights, store):
-        step = width // 2
-        partial = None
-        for x in range(0, width, step):
+        def products(x, step):
             left, right = [], []
             for dy in range(3):
                 for dx in range(3):
@@ -587,10 +578,7 @@
                         )
                         right.append(
                             jnp.concatenate(
-                                [
-                                    tap_block(weights, k - q, dy, dx, channels)
-                                    for q in range(2)
-                                ],
+                                [tap_block(weights, k - q, dy, dx, channels) for q in range(2)],
                                 axis=1,
                             )
                         )
@@ -599,19 +587,30 @@
                 jnp.concatenate(right, axis=0),
                 preferred_element_type=jnp.float32,
             )
+            sums = []
             for q in range(2):
                 tile = store(
-                    q, x, step, result[:, q * channels : (q + 1) * channels].reshape(
-                        step, both, channels
-                    )
+                    q,
+                    x,
+                    step,
+                    result[:, q * channels : (q + 1) * channels].reshape(step, both, channels),
                 )
                 tile = tile.astype(jnp.float32).reshape(-1, height, channels)
-                total, squares = jnp.sum(tile, axis=0), jnp.sum(tile * tile, axis=0)
-                if partial is None:
-                    partial = (total, squares)
-                else:
-                    partial = (partial[0] + total, partial[1] + squares)
-        return partial
+                sums.append((jnp.sum(tile, axis=0), jnp.sum(tile * tile, axis=0)))
+            return [sums[0][i] + sums[1][i] for i in range(2)]
+
+        step, piece = width // STEPS, width // PIECES
+        ready, partial = 0, None
+        border(0)
+        for x in range(0, width, step):
+            while ready < min(x + step + 1, width):
+                columns_at(ready, piece)
+                ready += piece
+                if ready == width:
+                    border(1)
+            sums = products(x, step)
+            partial = sums if partial is None else [partial[i] + sums[i] for i in range(2)]
+        return tuple(partial)
 
     def store_hidden(q, x, step, tile):
         tile = tile.astype(jnp.bfloat16)
@@ -643,25 +642,38 @@
         receive(0, values)
         moves_at("r", 0, layer)
         give(layer > 0)
-        activate(0, values, small[layer, 0:1], small[layer, 1:2])
         moves_at("b", 0, layer)
-        partial = convolution(kernels.at[2 * layer], store_hidden)
-        finish_sends(0, values)
+        partial = layer_half(
+            0,
+            values,
+            small[layer, 0:1],
+            small[layer, 1:2],
+            kernels.at[2 * layer],
+            store_hidden,
+        )
         take(layer > 0)
         exchange(1, hidden, partial)
+        finish_sends(0, values)
         moves_at("a", 1, layer)
         receive(1, hidden)
         moves_at("r", 1, layer)
         give(layer < layers - 1)
-        activate(1, hidden, small[layer, 2:3], small[layer, 3:4])
         moves_at("b", 1, layer)
-        partial = convolution(kernels.at[2 * layer + 1], store_values)
-        finish_sends(1, hidden)
+        partial = layer_half(
+            1,
+            hidden,
+            small[layer, 2:3],
+            small[layer, 3:4],
+            kernels.at[2 * layer + 1],
+            store_values,
+        )
 
         @pl.when(layer < layers - 1)
         def _():
             take(layer >= 0)
             exchange(0, values, partial)
+
+        finish_sends(1, hidden)
 
     for q in range(2):
         whole = values[q].astype(jnp.float32)
@@ -669,10 +681,6 @@
             turned[q + 2 * p] = whole[:, p * height : (p + 1) * height].reshape(
                 height * width, channels
             )
-    for f in range(frames):
-        for y in range(height):
-            staged[f, y] = turned[f, pl.ds(y, width, stride=height)].astype(jnp.bfloat16)
-
     def outgoing(k, me, to):
         return pltpu.make_async_remote_copy(
             src_ref=staged.at[:, pl.ds(to * local_rows, local_rows)],
@@ -683,8 +691,16 @@
             device_id_type=MESH,
         )
 
+    def stage(to):
+        for f in range(frames):
+            for i in range(local_rows):
+                y = to * local_rows + i
+                staged[f, y] = turned[f, pl.ds(y, width, stride=height)].astype(jnp.bfloat16)
+
     for k in range(1, count):
+        stage(lax.rem(row + k, count))
         outgoing(k, row, lax.rem(row + k, count)).start()
+    stage(row)
     own = pltpu.make_async_copy(
         staged.at[:, pl.ds(row * local_rows, local_rows)],
         out.at[0, :, :, pl.ds(pl.multiple_of(row * width, width), width)],

time: 71.5 us -> 70 us (0.979)
  Pallas kernels: 69.6 us -> 68.2 us
    pallas_call x1, Pallas kernels: 69.6 us -> 68.2 us  [body(): pl.pallas_call(functools.partial(decode_kernel, count), out_shape=jax.Sha...]
where the time goes in v5:
time: 70 us; the launch traced here: 69.9 us
  Pallas kernels  68.2 us (97%)
  local copies, waits for them, and re-layouts  1.67 us (2%)
    pallas_call x1, Pallas kernels, body(): pl.pallas_call(functools.partial(decode_kernel, count), out_shape=jax.Sha...  68.2 us
    unnamed x1, local copies, waits for them, and re-layouts  1.67 us

profile of v5, /device:TPU:0, one launch (start us, length us, event | category | flops | bytes accessed | tf_op | source)
XLA Modules:
  0.0 69.9 jit_solution(16206726032032262028)
XLA Ops:
  0.0 68.2 %shard_map.73 = bf16[1,4,2,128,128]{4,3,2,1,0:T(8,128)(2,1)} custom-call(bf16[4,4,2,128,128]{4,3,2,1,0:T(8,128)(2,1)} %latents.1, bf16[1,3,3,3,128,128]{5,4,3,2,1,0:T(8,128)(2,1)} %first.1, bf16[1,3,3,3,128,128]{5,4,3,2,1,0:T(8,128)(2,1)} %second.1, bf16[1,128]{1,0:T(2,128)(2,1)} %gain_first.1, bf16[1,128]{1,0:T(2,128)(2,1)} %bias_first.1, ...), custom_call_target="tpu_custom_call" | custom-call | tf_op jit(solution)/shard_map/pallas_call | solution.py:727
  68.2 1.7 %copy.9 = bf16[1,4,2,128,128]{4,3,2,1,0:T(8,128)(2,1)} copy(bf16[1,4,2,128,128]{4,3,2,1,0:T(8,128)(2,1)} %shard_map.73) | data formatting | bytes 524288

commit v6 on v5

--- a/solution.py
+++ b/solution.py
@@ -187,6 +187,9 @@
 
     given = (first, second)
     layers = kernels.shape[0] // 2
+    for k in (0, 3):
+        for dy in range(3):
+            active[k, dy, width + 2] = jnp.zeros((both, channels), jnp.bfloat16)
     depth = channels // 2
 
     def tensor_part(ref, half, chunk, chunks):
@@ -568,32 +571,58 @@
                     there,
                 )
 
+        def pixels(k, dy, x, step):
+            return active[k, dy, x : x + step].reshape(step * both, channels)
+
+        def lone(k, dt, x, step):
+            left, right = [], []
+            for dy in range(3):
+                left += [pixels(k, dy, x, step + 1), pixels(k, dy, x + 2, step + 1)]
+                for taps in ((0, 1), (2, None)):
+                    right.append(
+                        jnp.concatenate(
+                            [
+                                tap_block(weights, -1 if dx is None else dt, dy, dx, channels)
+                                for dx in taps
+                            ],
+                            axis=1,
+                        )
+                    )
+            part = jnp.dot(
+                jnp.concatenate(left, axis=1),
+                jnp.concatenate(right, axis=0),
+                preferred_element_type=jnp.float32,
+            )
+            return part[: step * both, :channels] + part[both:, channels:]
+
         def products(x, step):
             left, right = [], []
             for dy in range(3):
                 for dx in range(3):
-                    for k in (1, 2, 0, 3):
-                        left.append(
-                            active[k, dy, x + dx : x + dx + step].reshape(step * both, channels)
-                        )
+                    for k in (1, 2):
+                        left.append(pixels(k, dy, x + dx, step))
                         right.append(
                             jnp.concatenate(
                                 [tap_block(weights, k - q, dy, dx, channels) for q in range(2)],
                                 axis=1,
                             )
                         )
-            result = jnp.dot(
+            shared = jnp.dot(
                 jnp.concatenate(left, axis=1),
                 jnp.concatenate(right, axis=0),
                 preferred_element_type=jnp.float32,
             )
+            result = [
+                shared[:, :channels] + lone(0, 0, x, step),
+                shared[:, channels:] + lone(3, 2, x, step),
+            ]
             sums = []
             for q in range(2):
                 tile = store(
                     q,
                     x,
                     step,
-                    result[:, q * channels : (q + 1) * channels].reshape(step, both, channels),
+                    result[q].reshape(step, both, channels),
                 )
                 tile = tile.astype(jnp.float32).reshape(-1, height, channels)
                 sums.append((jnp.sum(tile, axis=0), jnp.sum(tile * tile, axis=0)))
@@ -737,7 +766,7 @@
             pltpu.VMEM((2, 2, width, both, channels), jnp.bfloat16),
             pltpu.VMEM((2, 2, 2, 2, both, channels), jnp.bfloat16),
             pltpu.VMEM((2, 2 * count, 8, channels), jnp.float32),
-            pltpu.VMEM((4, 3, width + 2, both, channels), jnp.bfloat16),
+            pltpu.VMEM((4, 3, width + 3, both, channels), jnp.bfloat16),
             dma,
             dma((count,)),
             dma((count,)),

time: 70 us -> 68.7 us (0.981)
  Pallas kernels: 68.2 us -> 66.8 us
    pallas_call x1, Pallas kernels: 68.2 us -> 66.8 us  [body(): pl.pallas_call(functools.partial(decode_kernel, count), out_shape=jax.Sha...]
where the time goes in v6:
time: 68.7 us; the launch traced here: 68.5 us
  Pallas kernels  66.8 us (97%)
  local copies, waits for them, and re-layouts  1.67 us (2%)
    pallas_call x1, Pallas kernels, body(): pl.pallas_call(functools.partial(decode_kernel, count), out_shape=jax.Sha...  66.8 us
    unnamed x1, local copies, waits for them, and re-layouts  1.67 us

profile of v6, /device:TPU:0, one launch (start us, length us, event | category | flops | bytes accessed | tf_op | source)
XLA Modules:
  0.0 68.5 jit_solution(8227243927239025185)
XLA Ops:
  0.0 66.8 %shard_map.73 = bf16[1,4,2,128,128]{4,3,2,1,0:T(8,128)(2,1)} custom-call(bf16[4,4,2,128,128]{4,3,2,1,0:T(8,128)(2,1)} %latents.1, bf16[1,3,3,3,128,128]{5,4,3,2,1,0:T(8,128)(2,1)} %first.1, bf16[1,3,3,3,128,128]{5,4,3,2,1,0:T(8,128)(2,1)} %second.1, bf16[1,128]{1,0:T(2,128)(2,1)} %gain_first.1, bf16[1,128]{1,0:T(2,128)(2,1)} %bias_first.1, ...), custom_call_target="tpu_custom_call" | custom-call | tf_op jit(solution)/shard_map/pallas_call | solution.py:756
  66.8 1.7 %copy.9 = bf16[1,4,2,128,128]{4,3,2,1,0:T(8,128)(2,1)} copy(bf16[1,4,2,128,128]{4,3,2,1,0:T(8,128)(2,1)} %shard_map.73) | data formatting | bytes 524288

commit v7 on v6

--- a/solution.py
+++ b/solution.py
@@ -198,7 +198,7 @@
         return ref.at[pl.ds(chunk * size, size), :, :, rows]
 
     def chunks_of(j):
-        return 3 if j < 2 else 1
+        return 3 if j < 4 else 1
 
     def remote_half(j, chunk, source, to, slot):
         return pltpu.make_async_remote_copy(
@@ -227,7 +227,7 @@
         route = routes[j]
         away = segment ^ (j // 2)
         source = given[j % 2].at[0]
-        each = range(chunks_of(j))
+        each = range(chunks_of(j)) if len(name) == 2 else (int(name[2]),)
         if route == "X":
             first_to = segment ^ 1
             second_to = pass_to = segment ^ 2
@@ -315,12 +315,12 @@
     plan = {
         "start": ("P0", "P2", "P4", "P6"),
         "early": ("Q1", "F0"),
-        "a0": ("P3", "F1", "R0"),
+        "a0": ("F1", "R0",),
         "r0": ("F2", "S2", "S4"),
         "b0": ("G0",),
         "a1": ("S3", "S6", "F4", "R1"),
         "b1": ("G1",),
-        "a2": ("F3", "P5", "R2", "F6"),
+        "a2": ("F32", "P5", "R2", "F6",),
         "b2": ("G2",),
         "a3": ("S5", "P7", "R4", "R3"),
         "r3": ("F5",),
@@ -332,6 +332,8 @@
         "r6": ("R7",),
         "b6": ("G6",),
         "b7": ("G7",),
+        "mid": ("P3",),
+        "r1": ("F30", "F31",),
         "end": ("W0", "W1", "W2", "W3", "W4", "W5", "W6", "W7"),
     }
 
@@ -404,9 +406,12 @@
     for k in range(1, count):
         other = lax.rem(row + k, count)
         incoming(k, other, row).wait_recv()
+    moves("mid")
 
     for f in range(frames):
-        turned[f] = staged[f].astype(jnp.float32).reshape(height * width, channels)
+        turned[f, : height * width] = (
+            staged[f].astype(jnp.float32).reshape(height * width, channels)
+        )
     zero = jnp.zeros((height, channels), jnp.float32)
 
     def turn(x, carry):
@@ -707,9 +712,9 @@
     for q in range(2):
         whole = values[q].astype(jnp.float32)
         for p in range(2):
-            turned[q + 2 * p] = whole[:, p * height : (p + 1) * height].reshape(
-                height * width, channels
-            )
+            turned[q + 2 * p, : height * width] = whole[
+                :, p * height : (p + 1) * height
+            ].reshape(height * width, channels)
     def outgoing(k, me, to):
         return pltpu.make_async_remote_copy(
             src_ref=staged.at[:, pl.ds(to * local_rows, local_rows)],
@@ -760,7 +765,7 @@
         out_specs=pl.BlockSpec(memory_space=pltpu.VMEM),
         scratch_shapes=[
             pltpu.VMEM((frames, height, width, channels), jnp.bfloat16),
-            pltpu.VMEM((frames, height * width, channels), jnp.float32),
+            pltpu.VMEM((frames, height * width + height + width, channels), jnp.float32),
             pltpu.VMEM((2, width, both, channels), jnp.bfloat16),
             pltpu.VMEM((2, width, both, channels), jnp.bfloat16),
             pltpu.VMEM((2, 2, width, both, channels), jnp.bfloat16),

time: 68.7 us -> 68.2 us (level)
  no operation moved by 1% of the time
where the time goes in v7:
time: 68.2 us; the launch traced here: 68 us
  Pallas kernels  66.3 us (97%)
  local copies, waits for them, and re-layouts  1.67 us (2%)
    pallas_call x1, Pallas kernels, body(): pl.pallas_call(functools.partial(decode_kernel, count), out_shape=jax.Sha...  66.3 us
    unnamed x1, local copies, waits for them, and re-layouts  1.67 us

profile of v7, /device:TPU:0, one launch (start us, length us, event | category | flops | bytes accessed | tf_op | source)
XLA Modules:
  0.0 68.0 jit_solution(2272365037654696721)
XLA Ops:
  0.0 66.3 %shard_map.73 = bf16[1,4,2,128,128]{4,3,2,1,0:T(8,128)(2,1)} custom-call(bf16[4,4,2,128,128]{4,3,2,1,0:T(8,128)(2,1)} %latents.1, bf16[1,3,3,3,128,128]{5,4,3,2,1,0:T(8,128)(2,1)} %first.1, bf16[1,3,3,3,128,128]{5,4,3,2,1,0:T(8,128)(2,1)} %second.1, bf16[1,128]{1,0:T(2,128)(2,1)} %gain_first.1, bf16[1,128]{1,0:T(2,128)(2,1)} %bias_first.1, ...), custom_call_target="tpu_custom_call" | custom-call | tf_op jit(solution)/shard_map/pallas_call | solution.py:761
  66.3 1.7 %copy.9 = bf16[1,4,2,128,128]{4,3,2,1,0:T(8,128)(2,1)} copy(bf16[1,4,2,128,128]{4,3,2,1,0:T(8,128)(2,1)} %shard_map.73) | data formatting | bytes 524288

commit v8 on v7

--- a/solution.py
+++ b/solution.py
@@ -318,7 +318,7 @@
         "a0": ("F1", "R0",),
         "r0": ("F2", "S2", "S4"),
         "b0": ("G0",),
-        "a1": ("S3", "S6", "F4", "R1"),
+        "a1": ("S3", "F4", "F30", "R1",),
         "b1": ("G1",),
         "a2": ("F32", "P5", "R2", "F6",),
         "b2": ("G2",),
@@ -333,7 +333,7 @@
         "b6": ("G6",),
         "b7": ("G7",),
         "mid": ("P3",),
-        "r1": ("F30", "F31",),
+        "r1": ("S6", "F31",),
         "end": ("W0", "W1", "W2", "W3", "W4", "W5", "W6", "W7"),
     }
 
@@ -426,9 +426,7 @@
             squares = squares + tile[:height] + tile[height:]
         return total, squares
 
-    partial = lax.fori_loop(0, width, turn, (zero, zero), unroll=4)
-    for k in range(1, count):
-        incoming(k, row, lax.rem(row + k, count)).wait_send()
+    partial = lax.fori_loop(0, width, turn, (zero, zero), unroll=16)
 
     def stat_copy(par, k, me, to, tm_from, tm_to):
         slot = tm_from * count + me
@@ -667,6 +665,8 @@
             pl.semaphore_wait(free_sem, 1)
 
     exchange(0, values, partial)
+    for k in range(1, count):
+        incoming(k, row, lax.rem(row + k, count)).wait_send()
     for k in range(1, 4):
         param_copy(k, segment ^ k).wait_recv()
 

time: 68.2 us -> 68 us (level)
  no operation moved by 1% of the time
where the time goes in v8:
time: 68 us; the launch traced here: 67.5 us
  Pallas kernels  65.9 us (97%)
  local copies, waits for them, and re-layouts  1.67 us (2%)
    pallas_call x1, Pallas kernels, body(): pl.pallas_call(functools.partial(decode_kernel, count), out_shape=jax.Sha...  65.9 us
    unnamed x1, local copies, waits for them, and re-layouts  1.67 us

profile of v8, /device:TPU:0, one launch (start us, length us, event | category | flops | bytes accessed | tf_op | source)
XLA Modules:
  0.0 67.5 jit_solution(12952829741698534267)
XLA Ops:
  0.0 65.9 %shard_map.73 = bf16[1,4,2,128,128]{4,3,2,1,0:T(8,128)(2,1)} custom-call(bf16[4,4,2,128,128]{4,3,2,1,0:T(8,128)(2,1)} %latents.1, bf16[1,3,3,3,128,128]{5,4,3,2,1,0:T(8,128)(2,1)} %first.1, bf16[1,3,3,3,128,128]{5,4,3,2,1,0:T(8,128)(2,1)} %second.1, bf16[1,128]{1,0:T(2,128)(2,1)} %gain_first.1, bf16[1,128]{1,0:T(2,128)(2,1)} %bias_first.1, ...), custom_call_target="tpu_custom_call" | custom-call | tf_op jit(solution)/shard_map/pallas_call | solution.py:761
  65.9 1.7 %copy.9 = bf16[1,4,2,128,128]{4,3,2,1,0:T(8,128)(2,1)} copy(bf16[1,4,2,128,128]{4,3,2,1,0:T(8,128)(2,1)} %shard_map.73) | data formatting | bytes 524288

commit v9 on v8

--- a/solution.py
+++ b/solution.py
@@ -320,20 +320,21 @@
         "b0": ("G0",),
         "a1": ("S3", "F4", "F30", "R1",),
         "b1": ("G1",),
-        "a2": ("F32", "P5", "R2", "F6",),
+        "a2": ("P7", "F32", "R2", "F6",),
         "b2": ("G2",),
-        "a3": ("S5", "P7", "R4", "R3"),
-        "r3": ("F5",),
+        "a3": ("F5", "R4", "R3",),
         "b3": ("G3",),
-        "a4": ("S7", "R6"),
+        "a4": ("F7", "R6",),
         "b4": ("G4",),
-        "a5": ("F7", "R5"),
+        "a5": ("R5",),
         "b5": ("G5",),
         "r6": ("R7",),
         "b6": ("G6",),
         "b7": ("G7",),
         "mid": ("P3",),
-        "r1": ("S6", "F31",),
+        "r1": ("P5", "S6", "F31",),
+        "r2": ("S5",),
+        "r3": ("S7",),
         "end": ("W0", "W1", "W2", "W3", "W4", "W5", "W6", "W7"),
     }
 

time: 68 us -> 68 us (level)
  no operation moved by 1% of the time
where the time goes in v9:
time: 68 us; the launch traced here: 67 us
  Pallas kernels  65.3 us (96%)
  local copies, waits for them, and re-layouts  1.67 us (2%)
    pallas_call x1, Pallas kernels, body(): pl.pallas_call(functools.partial(decode_kernel, count), out_shape=jax.Sha...  65.3 us
    unnamed x1, local copies, waits for them, and re-layouts  1.67 us

profile of v9, /device:TPU:0, one launch (start us, length us, event | category | flops | bytes accessed | tf_op | source)
XLA Modules:
  0.0 67.0 jit_solution(6839058291187985897)
XLA Ops:
  0.0 65.3 %shard_map.73 = bf16[1,4,2,128,128]{4,3,2,1,0:T(8,128)(2,1)} custom-call(bf16[4,4,2,128,128]{4,3,2,1,0:T(8,128)(2,1)} %latents.1, bf16[1,3,3,3,128,128]{5,4,3,2,1,0:T(8,128)(2,1)} %first.1, bf16[1,3,3,3,128,128]{5,4,3,2,1,0:T(8,128)(2,1)} %second.1, bf16[1,128]{1,0:T(2,128)(2,1)} %gain_first.1, bf16[1,128]{1,0:T(2,128)(2,1)} %bias_first.1, ...), custom_call_target="tpu_custom_call" | custom-call | tf_op jit(solution)/shard_map/pallas_call | solution.py:762
  65.3 1.7 %copy.9 = bf16[1,4,2,128,128]{4,3,2,1,0:T(8,128)(2,1)} copy(bf16[1,4,2,128,128]{4,3,2,1,0:T(8,128)(2,1)} %shard_map.73) | data formatting | bytes 524288
